TPU v7x, 32 devices: a whole 2x2x4 slice. The times are simulated.
32 devices in a mesh: groups: 2 (over y), blk: 8 (over z, x), uly: 2 (over core).
Axes of the slice: x: 2, y: 2, z: 4, core: 2. Of those that a mesh axis runs over, the one named last changes fastest.
Arguments:
- query_proj: bfloat16 [4096, 4096], P(('groups', 'blk', 'uly')), parts along dimension 0, may hold values from -17 to 17
- key_proj: bfloat16 [4096, 512], P(('groups', 'blk', 'uly')), parts along dimension 0, may hold values from -17 to 17
- value_projection: bfloat16 [4096, 512], P(('groups', 'blk', 'uly')), parts along dimension 0, may hold values from -6 to 6
- query_gain: float32 [128], replicated, may hold values from 0.5 to 6
- key_gain: float32 [128], replicated, may hold values from 0.5 to 6
Outputs:
- attended: bfloat16 [4096, 4096], P(('groups', 'blk', 'uly')), parts along dimension 0
There are 2 independent parts, one for each index of `groups`. A program takes and returns all parts, laid end to end along the dimension named above; an argument that names none is the same for every part. Nothing has to cross between parts.
All inputs are finite; a program needn't handle non-finite values.
Results may differ from a plain program's by a relative error of at most 0.0085.
The roundings to bfloat16 on the way count: a program that leaves them out, or rounds other values in their place, can miss the bound.
Values may be sent and summed in bfloat16 or wider, within the bound.
No kernel may reach another device: no remote copies, remote signals or barrier semaphores. Data moves between devices by JAX's collectives and lax.ppermute only.
A program may use at most 64 MiB of HBM per device.

v0:
```python
import math

import jax
import jax.numpy as jnp
from jax import lax
from jax.sharding import PartitionSpec as P

NEG_FILL = -1e30
ROPE_BASE = 1000000.0


def shifted(block, axis, distance):
    devices = range(lax.axis_size(axis))
    route = [(i - distance, i) for i in devices if i - distance in devices]
    return lax.ppermute(block, axis, route)


def rotate_rows(source, scales, positions):
    head_width = scales.shape[0]
    row_count = source.shape[0]
    head_count = source.shape[1] // head_width
    values = source.astype(jnp.float32).reshape(row_count, head_count, head_width)
    mean_square = jnp.mean(values * values, axis=-1, keepdims=True)
    normed = values * lax.rsqrt(mean_square + 1e-06) * scales
    half_width = head_width // 2
    frequency = jnp.exp(
        jnp.arange(half_width, dtype=jnp.float32) * (-2.0 * math.log(ROPE_BASE) / head_width)
    )
    angles = positions.astype(jnp.float32)[:, None] * frequency[None, :]
    cosine = jnp.cos(angles)[:, None, :]
    sine = jnp.sin(angles)[:, None, :]
    first_half = normed[..., :half_width]
    second_half = normed[..., half_width:]
    rotated = jnp.concatenate(
        [first_half * cosine - second_half * sine, second_half * cosine + first_half * sine],
        axis=-1,
    )
    return rotated.reshape(row_count, head_count * head_width).astype(jnp.bfloat16)


def attend(running, query_rows, query_pos, key_rows, value_rows, key_pos, key_valid, window):
    top_score, total_weight, weighted = running
    row_count = query_rows.shape[0]
    key_count = key_rows.shape[0]
    head_width = weighted.shape[-1]
    kv_heads = key_rows.shape[1] // head_width
    group_count = query_rows.shape[1] // head_width // kv_heads
    query_heads = query_rows.reshape(row_count, kv_heads, group_count, head_width)
    key_heads = key_rows.reshape(key_count, kv_heads, head_width)
    value_heads = value_rows.reshape(key_count, kv_heads, head_width)
    scores = jnp.einsum(
        "rkgd,nkd->kgrn", query_heads, key_heads, preferred_element_type=jnp.float32
    ) * (1.0 / math.sqrt(head_width))
    distance = query_pos[:, None] - key_pos[None, :]
    allowed = (distance >= 0) & (distance < window) & key_valid[None, :]
    scores = jnp.where(allowed, scores, NEG_FILL)
    new_top = jnp.maximum(top_score, jnp.max(scores, axis=-1))
    weights = jnp.exp(scores - new_top[..., None])
    rescale = jnp.exp(top_score - new_top)
    total_weight = total_weight * rescale + jnp.sum(weights, axis=-1)
    weighted = weighted * rescale[..., None] + jnp.einsum(
        "kgrn,nkd->kgrd",
        weights.astype(jnp.bfloat16),
        value_heads,
        preferred_element_type=jnp.float32,
    )
    return (new_top, total_weight, weighted)


def finish(running):
    top_score, total_weight, weighted = running
    mixed_rows = weighted / total_weight[..., None]
    return (
        jnp.transpose(mixed_rows, (2, 0, 1, 3))
        .reshape(mixed_rows.shape[2], -1)
        .astype(jnp.bfloat16)
    )


def local(query_proj, key_proj, value_projection, query_gain, key_gain):
    cycle_size = lax.axis_size("blk")
    cycle_index = lax.axis_index("blk")
    stretch_len = query_proj.shape[0]
    head_width = query_gain.shape[0]
    span_steps = max(1, cycle_size // 64)
    window = span_steps * stretch_len
    last_stretch = 2 * cycle_size - 1
    offsets = jnp.arange(stretch_len, dtype=jnp.int32)
    low_pos = cycle_index * stretch_len + offsets
    high_pos = (last_stretch - cycle_index) * stretch_len + offsets
    both_pos = jnp.concatenate([low_pos, high_pos])
    query_raw, key_raw, value_all = (
        lax.all_to_all(query_proj, "uly", split_axis=1, concat_axis=0, tiled=True),
        lax.all_to_all(key_proj, "uly", split_axis=1, concat_axis=0, tiled=True),
        lax.all_to_all(value_projection, "uly", split_axis=1, concat_axis=0, tiled=True),
    )
    query_all = rotate_rows(query_raw, query_gain, both_pos)
    key_all = rotate_rows(key_raw, key_gain, both_pos)
    query_low = query_all[:stretch_len]
    query_high = query_all[stretch_len:]
    kv_heads = key_all.shape[1] // head_width
    group_count = query_all.shape[1] // head_width // kv_heads

    def fresh_state():
        return (
            jnp.full((kv_heads, group_count, stretch_len), NEG_FILL, jnp.float32),
            jnp.zeros((kv_heads, group_count, stretch_len), jnp.float32),
            jnp.zeros((kv_heads, group_count, stretch_len, head_width), jnp.float32),
        )

    low_state = attend(
        fresh_state(),
        query_low,
        low_pos,
        key_all[:stretch_len],
        value_all[:stretch_len],
        low_pos,
        jnp.ones((stretch_len,), bool),
        window,
    )
    high_state = attend(
        fresh_state(),
        query_high,
        high_pos,
        key_all,
        value_all,
        both_pos,
        jnp.ones((2 * stretch_len,), bool),
        window,
    )
    block_pair = jnp.stack([key_all, value_all])

    def send_up(payload):
        return shifted(payload, "blk", 1)

    upward = block_pair[:, :stretch_len]

    def cycle_turn(offset, carried):
        upward, downward, low_state, high_state = carried
        upward = send_up(upward)
        downward = shifted(downward, "blk", -1)
        left_index = cycle_index - offset
        right_index = cycle_index + offset
        left_pos = left_index * stretch_len + offsets
        right_low = right_index * stretch_len + offsets
        right_high = (last_stretch - right_index) * stretch_len + offsets
        left_valid = jnp.broadcast_to(left_index >= 0, (stretch_len,))
        right_valid = jnp.broadcast_to(right_index <= cycle_size - 1, (2 * stretch_len,))
        left_keys = upward[0, :stretch_len]
        left_values = upward[1, :stretch_len]
        low_state = attend(
            low_state, query_low, low_pos, left_keys, left_values, left_pos, left_valid, window
        )
        high_keys = jnp.concatenate([left_keys, downward[0]])
        high_values = jnp.concatenate([left_values, downward[1]])
        high_key_pos = jnp.concatenate([left_pos, right_low, right_high])
        high_valid = jnp.concatenate([left_valid, right_valid])
        high_state = attend(
            high_state,
            query_high,
            high_pos,
            high_keys,
            high_values,
            high_key_pos,
            high_valid,
            window,
        )
        return (upward, downward, low_state, high_state)

    carried = lax.fori_loop(
        1, span_steps + 1, cycle_turn, (upward, block_pair, low_state, high_state)
    )
    merged = jnp.concatenate([finish(carried[2]), finish(carried[3])])
    return lax.all_to_all(merged, "uly", split_axis=0, concat_axis=1, tiled=True)


def solution(mesh):
    placed = (
        P(("groups", "blk", "uly"), None),
        P(("groups", "blk", "uly"), None),
        P(("groups", "blk", "uly"), None),
        P(),
        P(),
    )
    return jax.shard_map(
        local,
        mesh=mesh,
        in_specs=placed,
        out_specs=P(("groups", "blk", "uly"), None),
        check_vma=False,
    )
```

profile of v0, /device:TPU:13, one launch (start us, length us, event | category | flops | bytes accessed | tf_op | source)
XLA Modules:
  0.0 51.0 jit_solution(1183035205590962859)
XLA Ops:
  0.0 1.6 %copy.156 = bf16[16,2,8,256]{3,2,0,1:T(8,128)(2,1)} copy(bf16[16,2,8,256]{3,2,1,0:T(8,128)(2,1)} %bitcast.194) | data formatting | bytes 262144 | tf_op jit(solution)/shard_map/all_to_all | solution.py:94
  1.6 4.0 %all-to-all-start = ((bf16[128,2,256]{2,0,1:T(8,128)(2,1)}), bf16[128,2,256]{2,0,1:T(8,128)(2,1)S(1)}, u32[]{:S(2)}, u32[]{:S(2)}) async-start(bf16[128,2,256]{2,0,1:T(8,128)(2,1)} %bitcast.172), calls=%async_computation | async-start | bytes 262144 | tf_op jit(solution)/shard_map/all_to_all | solution.py:94
  5.6 1.7 %copy.117 = bf16[128,512]{0,1:T(8,128)(2,1)} copy(bf16[128,512]{1,0:T(8,128)(2,1)} %param.7) | data formatting | bytes 262144 | tf_op args[2]
  7.3 0.0 all-to-all-done
  7.3 3.4 %all-to-all-start.2 = ((bf16[128,2,256]{0,2,1:T(8,128)(2,1)}), bf16[128,2,256]{0,2,1:T(8,128)(2,1)S(1)}, u32[]{:S(2)}, u32[]{:S(2)}) async-start(bf16[128,2,256]{0,2,1:T(8,128)(2,1)} %bitcast.7), calls=%async_computation.2 | async-start | bytes 262144 | tf_op jit(solution)/shard_map/all_to_all | solution.py:95
  10.7 0.1 reshape.245
  10.9 0.3 multiply_reduce_fusion.1
  11.2 0.1 copy.111
  11.3 0.5 %multiply_cosine_fusion = (f32[256,64]{1,0:T(8,128)S(1)}, f32[256,64]{1,0:T(8,128)S(1)}) fusion(f32[64]{0:T(128)S(1)} %multiply_exponential_fusion, f32[256]{0:T(256)S(1)} %get-tuple-element.76), kind=kLoop, calls=%fused_computation.77 | loop fusion | flops 16384 | bytes 132352 | tf_op jit(solution)/shard_map/cos | solution.py:30
  11.9 0.1 fusion.39
  12.0 0.2 multiply_subtract_fusion
  12.2 0.1 maximum_convert_fusion
  12.3 0.1 copy.119
  12.4 0.0 all-to-all-done.2
  12.4 0.1 copy.120
  12.6 0.1 copy.121
  12.7 0.7 %fusion.47 = bf16[2,128,256]{1,2,0:T(8,128)(2,1)} fusion(bf16[1,256,256]{1,2,0:T(8,128)(2,1)S(1)} %bitcast.184, bf16[1,256,256]{1,2,0:T(8,128)(2,1)S(1)} %copy.121), kind=kLoop, calls=%fused_computation.78 | loop fusion | flops 65536 | bytes 393216 | tf_op jit(solution)/shard_map/stack | solution.py:131
  13.3 3.1 %collective-permute-start = (bf16[2,128,256]{1,2,0:T(8,128)(2,1)}, bf16[2,128,256]{1,2,0:T(8,128)(2,1)}, u32[]{:S(2)}, u32[]{:S(2)}) collective-permute-start(bf16[2,128,256]{1,2,0:T(8,128)(2,1)} %fusion.47), channel_id=1, source_target_pairs={{0,2},{2,4},{4,6},{6,8},{8,10},{10,12},{12,14},{1,3},{3,5},{5,7},{... | collective-permute-start | bytes 393224 | tf_op jit(solution)/shard_map/while/body/eval_jaxpr/ppermute | solution.py:15
  16.4 2.3 %copy.155 = bf16[16,2,8,2048]{3,2,0,1:T(8,128)(2,1)} copy(bf16[16,2,8,2048]{3,2,1,0:T(8,128)(2,1)} %bitcast.186) | data formatting | bytes 2097152 | tf_op jit(solution)/shard_map/all_to_all | solution.py:93
  18.8 3.9 %all-to-all-start.1 = ((bf16[128,2,2048]{2,0,1:T(8,128)(2,1)}), bf16[128,2,2048]{2,0,1:T(8,128)(2,1)S(1)}, u32[]{:S(2)}, u32[]{:S(2)}) async-start(bf16[128,2,2048]{2,0,1:T(8,128)(2,1)} %bitcast.171), calls=%async_computation.1 | async-start | bytes 2097152 | tf_op jit(solution)/shard_map/all_to_all | solution.py:93
  22.6 0.7 %pad_maximum_fusion.2 = bf16[2,256,256]{1,2,0:T(8,128)(2,1)} fusion(bf16[1,256,256]{1,2,0:T(8,128)(2,1)S(1)} %copy.121, bf16[1,256,256]{1,2,0:T(8,128)(2,1)S(1)} %bitcast.185), kind=kLoop, calls=%fused_computation.54 | loop fusion | flops 131072 | bytes 524288 | tf_op jit(solution)/shard_map/stack | solution.py:131
  23.4 3.1 %collective-permute-start.1 = (bf16[2,256,256]{1,2,0:T(8,128)(2,1)}, bf16[2,256,256]{1,2,0:T(8,128)(2,1)}, u32[]{:S(2)}, u32[]{:S(2)}) collective-permute-start(bf16[2,256,256]{1,2,0:T(8,128)(2,1)} %pad_maximum_fusion.2), channel_id=1, source_target_pairs={{2,0},{4,2},{6,4},{8,6},{10,8},{12,10},{14,12},{3,1},{5,3},{7,5},{... | collective-permute-start | bytes 786440 | tf_op jit(solution)/shard_map/while/body/eval_jaxpr/ppermute | solution.py:15
  26.4 0.1 copy.125
  26.6 0.0 all-to-all-done.1
  26.6 0.2 convert_element_type.91
  26.8 0.4 copy.149
  27.2 0.0 copy-start.7
  27.2 0.6 %multiply_reduce_fusion = f32[256,16]{1,0:T(8,128)S(1)} fusion(f32[256,16,128]{2,1,0:T(8,128)S(1)} %bitcast.173), kind=kLoop, calls=%fused_computation.10 | loop fusion | flops 1044480 | bytes 2113536 | tf_op jit(solution)/shard_map/reduce_sum | solution.py:23
  27.9 0.1 copy.114
  27.9 0.1 copy.115
  28.1 0.9 %multiply_multiply_fusion = f32[256,16,128]{2,1,0:T(8,128)S(1)} fusion(f32[128]{0:T(128)S(1)} %copy-done.7, f32[256,16]{1,0:T(8,128)S(1)} %copy.115, f32[32,8,16,128]{3,2,1,0:T(8,128)S(1)} %copy.149), kind=kLoop, calls=%fused_computation.9 | loop fusion | flops 1048576 | bytes 4211200 | tf_op jit(solution)/shard_map/mul | solution.py:24
  28.9 0.8 %subtract_convert_fusion = (bf16[256,16,64]{2,1,0:T(8,128)(2,1)S(1)}, bf16[256,16,64]{2,1,0:T(8,128)(2,1)S(1)}) fusion(f32[256,16,128]{2,1,0:T(8,128)S(1)} %multiply_multiply_fusion, f32[256,64]{1,0:T(8,128)S(1)} %get-tuple-element.74, f32[256,64]{1,0:T(8,128)S(1)} %get-tuple-element.73), kind=kLoop, calls=%fused_computation.8 | loop fusion | flops 2097152 | bytes 3276800 | tf_op jit(solution)/shard_map/convert.4
  29.7 0.6 %fusion.36 = (bf16[128,16,128]{2,1,0:T(8,128)(2,1)S(1)}, bf16[128,16,128]{2,1,0:T(8,128)(2,1)S(1)}) fusion(bf16[256,16,64]{2,1,0:T(8,128)(2,1)S(1)} %get-tuple-element.39, bf16[256,16,64]{2,1,0:T(8,128)(2,1)S(1)} %get-tuple-element.40), kind=kLoop, calls=%fused_computation.49 | loop fusion | flops 2097152 | bytes 2097152 | tf_op jit(solution)/shard_map/concatenate | solution.py:34
  30.3 0.1 copy.116
  30.5 0.9 %copy.124 = bf16[128,16,128]{2,0,1:T(8,128)(2,1)} copy(bf16[128,16,128]{2,1,0:T(8,128)(2,1)S(1)} %get-tuple-element.42) | data formatting | bytes 1048576 | tf_op jit(solution)/shard_map/slice | solution.py:100
  31.4 0.1 fusion.50
  31.5 0.7 %reshape.252 = bf16[256,2,128,1]{0,2,1,3:T(8,128)(2,1)} reshape(bf16[2,128,256]{1,0,2:T(2,128)(2,1)S(1)} %copy.125) | data formatting | bytes 262144 | tf_op jit(solution)/shard_map/reshape | solution.py:50
  32.2 0.1 fusion.53
  32.4 0.3 fusion.74
  32.7 1.5 %fusion.73 = (f32[2,8,128]{2,1,0:T(8,128)S(1)}, f32[2,8,128,256]{2,3,1,0:T(8,128)S(1)}) fusion(bf16[128,2,8,128]{3,0,2,1:T(8,128)(2,1)} %bitcast.177, bf16[256,2,128]{2,0,1:T(8,128)(2,1)S(1)} %maximum_convert_fusion, pred[128,256]{0,1:T(8,128)(4,1)S(1)} %fusion.50), kind=kOutput, calls=%fused_computation.128 | convolution fusion | flops 135788544 | bytes 2793472 | tf_op jit(solution)/shard_map/rkgd,nkd->kgrn/dot_general | solution.py:51
  34.2 0.2 fusion.46
  34.4 0.0 collective-permute-done
  34.4 1.5 %fusion.72 = (bf16[1,128,256]{1,2,0:T(8,128)(2,1)}, bf16[1,128,256]{1,2,0:T(8,128)(2,1)S(1)}) fusion(bf16[2,128,256]{1,2,0:T(8,128)(2,1)} %collective-permute-done), kind=kLoop, calls=%fused_computation.127 | loop fusion | bytes 262144 | tf_op jit(solution)/shard_map/while/body/eval_jaxpr/slice | solution.py:150
  35.9 0.1 copy.127
  36.1 1.4 %fusion.75 = (f32[2,8,128]{2,1,0:T(8,128)S(1)}, f32[2,8,128,128]{2,3,1,0:T(8,128)S(1)}) fusion(bf16[128,2,128,1]{0,2,3,1:T(8,128)(2,1)S(1)} %bitcast.188, bf16[128,2,8,128]{3,0,2,1:T(8,128)(2,1)} %bitcast.176, pred[128,128]{0,1:T(8,128)(4,1)S(1)} %get-tuple-element.77), kind=kOutput, calls=%fused_computation.130 | convolution fusion | flops 67893248 | bytes 1662976 | tf_op jit(solution)/shard_map/while/body/eval_jaxpr/rkgd,nkd->kgrn/dot_general | solution.py:51
  37.5 0.2 fusion.30
  37.7 0.2 fusion.32
  37.9 0.3 fusion.16
  38.2 0.1 copy-done.4
  38.3 0.3 fusion.26
  38.7 0.0 collective-permute-done.1
  38.7 1.6 %fusion.71 = (bf16[1,256,256]{1,2,0:T(8,128)(2,1)}, bf16[1,256,256]{1,2,0:T(8,128)(2,1)S(1)}) fusion(bf16[2,256,256]{1,2,0:T(8,128)(2,1)} %collective-permute-done.1), kind=kLoop, calls=%fused_computation.126 | loop fusion | bytes 524288 | tf_op jit(solution)/shard_map/while/body/eval_jaxpr/slice | solution.py:155
  40.3 0.1 copy.128
  40.4 0.6 %fusion.2 = (f32[2,8,128]{2,1,0:T(8,128)S(1)}, f32[2,384,128,8]{2,1,3,0:T(8,128)S(1)}) fusion(pred[128,384]{0,1:T(8,128)(4,1)S(1)} %fusion.46, bf16[128,2,8,128]{3,0,2,1:T(8,128)(2,1)S(1)} %bitcast.178, bf16[256,2,128]{2,0,1:T(8,128)(2,1)S(1)} %copy.128, bf16[128,2,128]{2,0,1:T(8,128)(2,1)S(1)} %copy.127), kind=kOutput, calls=%fused_computation.4 | convolution fusion | flops 204077056 | bytes 3923968 | tf_op jit(solution)/shard_map/while/body/eval_jaxpr/rkgd,nkd->kgrn/dot_general | solution.py:51
  41.1 0.3 fusion.3
  41.4 0.7 %fusion = f32[2,8,128]{2,1,0:T(8,128)S(1)} fusion(f32[2,384,128,8]{2,1,3,0:T(8,128)S(1)} %get-tuple-element.82, f32[2,8,128]{2,1,0:T(8,128)S(1)} %get-tuple-element.72, pred[128,384]{0,1:T(8,128)(4,1)S(1)} %fusion.46), kind=kLoop, calls=%fused_computation.2 | loop fusion | flops 3143680 | bytes 3211264 | tf_op jit(solution)/shard_map/while/body/eval_jaxpr/reduce_sum | solution.py:60
  42.1 0.2 copy-done.3
  42.3 0.9 %fusion.19 = f32[128,2,8,128]{0,3,2,1:T(8,128)S(1)} fusion(f32[2,384,128,8]{2,1,3,0:T(8,128)S(1)} %get-tuple-element.82, f32[2,8,128]{2,1,0:T(8,128)S(1)} %get-tuple-element.72, pred[128,384]{0,1:T(8,128)(4,1)S(1)} %fusion.46, bf16[256,2,128]{0,2,1:T(8,128)(2,1)S(1)} %bitcast.195, bf16[128,2,128]{0,2,1:T(8,128)(2,1)S(1)} %bitcast.197), kind=kOutput, calls=%fused_computation.29 | convolution fusion | flops 204865536 | bytes 4448256 | tf_op jit(solution)/shard_map/while/body/eval_jaxpr/kgrn,nkd->kgrd/dot_general | solution.py:61
  43.2 0.5 %fusion.27 = bf16[128,2,8,128]{0,3,2,1:T(8,128)(2,1)S(1)} fusion(f32[128,2,8,128]{0,3,2,1:T(8,128)S(1)} %fusion.19, f32[2,8,128,256]{2,3,1,0:T(8,128)S(1)} %get-tuple-element.80, f32[2,8,128]{2,1,0:T(8,128)S(1)} %get-tuple-element.71, f32[128,2,8]{0,2,1:T(8,128)S(1)} %get-tuple-element.37, f32[128,2,8]{0,2,1:T(8,128)S(1)} %get-tuple-element.38, ...), kind=kOutput, calls=%fused_computation.37 | convolution fusion | flops 136577024 | bytes 3833856 | tf_op jit(solution)/shard_map/kgrn,nkd->kgrd/dot_general | solution.py:61
  43.7 0.1 pad_maximum_fusion
  43.9 0.6 %copy.130 = bf16[256,2048]{1,0:T(8,128)(2,1)S(1)} copy(bf16[256,2048]{0,1:T(8,128)(2,1)S(1)} %pad_maximum_fusion) | data formatting | bytes 2097152 | tf_op jit(solution)/shard_map/concatenate | solution.py:173
  44.5 4.5 %all_to_all.61 = bf16[2,128,2048]{2,1,0:T(8,128)(2,1)S(1)} all-to-all(bf16[2,128,2048]{2,1,0:T(8,128)(2,1)S(1)} %bitcast.179), channel_id=1, replica_groups=mesh['groups'=2,'blk'=8,'uly'=2] {'uly'}, dimensions={0} | all-to-all | bytes 2097152 | tf_op jit(solution)/shard_map/all_to_all | solution.py:174
  49.0 0.7 %copy.131 = bf16[2,128,2048]{1,2,0:T(8,128)(2,1)S(1)} copy(bf16[2,128,2048]{2,1,0:T(8,128)(2,1)S(1)} %all_to_all.61) | data formatting | bytes 2097152 | tf_op jit(solution)/shard_map/all_to_all | solution.py:174
  49.7 1.3 %copy.132 = bf16[128,4096]{1,0:T(8,128)(2,1)} copy(bf16[128,4096]{0,1:T(8,128)(2,1)S(1)} %bitcast.180) | data formatting | bytes 2097152 | tf_op jit(solution)/shard_map/all_to_all | solution.py:174
  (29 shorter events, 0.2 us)
Async XLA Ops:
  0.0 11.9 %copy-start.6 = (f32[128]{0:T(128)S(1)}, f32[128]{0:T(128)}, u32[]{:S(2)}) copy-start(f32[128]{0:T(128)} %param.9) | copy-start | bytes 1540
  1.6 5.7 %all-to-all-start = ((bf16[128,2,256]{2,0,1:T(8,128)(2,1)}), bf16[128,2,256]{2,0,1:T(8,128)(2,1)S(1)}, u32[]{:S(2)}, u32[]{:S(2)}) async-start(bf16[128,2,256]{2,0,1:T(8,128)(2,1)} %bitcast.172), calls=%async_computation | async-start | bytes 262144 | tf_op jit(solution)/shard_map/all_to_all | solution.py:94
  7.3 5.1 %all-to-all-start.2 = ((bf16[128,2,256]{0,2,1:T(8,128)(2,1)}), bf16[128,2,256]{0,2,1:T(8,128)(2,1)S(1)}, u32[]{:S(2)}, u32[]{:S(2)}) async-start(bf16[128,2,256]{0,2,1:T(8,128)(2,1)} %bitcast.7), calls=%async_computation.2 | async-start | bytes 262144 | tf_op jit(solution)/shard_map/all_to_all | solution.py:95
  13.3 21.1 %collective-permute-start = (bf16[2,128,256]{1,2,0:T(8,128)(2,1)}, bf16[2,128,256]{1,2,0:T(8,128)(2,1)}, u32[]{:S(2)}, u32[]{:S(2)}) collective-permute-start(bf16[2,128,256]{1,2,0:T(8,128)(2,1)} %fusion.47), channel_id=1, source_target_pairs={{0,2},{2,4},{4,6},{6,8},{8,10},{10,12},{12,14},{1,3},{3,5},{5,7},{... | collective-permute-start | bytes 393224 | tf_op jit(solution)/shard_map/while/body/eval_jaxpr/ppermute | solution.py:15
  18.8 7.8 %all-to-all-start.1 = ((bf16[128,2,2048]{2,0,1:T(8,128)(2,1)}), bf16[128,2,2048]{2,0,1:T(8,128)(2,1)S(1)}, u32[]{:S(2)}, u32[]{:S(2)}) async-start(bf16[128,2,2048]{2,0,1:T(8,128)(2,1)} %bitcast.171), calls=%async_computation.1 | async-start | bytes 2097152 | tf_op jit(solution)/shard_map/all_to_all | solution.py:93
  23.4 15.3 %collective-permute-start.1 = (bf16[2,256,256]{1,2,0:T(8,128)(2,1)}, bf16[2,256,256]{1,2,0:T(8,128)(2,1)}, u32[]{:S(2)}, u32[]{:S(2)}) collective-permute-start(bf16[2,256,256]{1,2,0:T(8,128)(2,1)} %pad_maximum_fusion.2), channel_id=1, source_target_pairs={{2,0},{4,2},{6,4},{8,6},{10,8},{12,10},{14,12},{3,1},{5,3},{7,5},{... | collective-permute-start | bytes 786440 | tf_op jit(solution)/shard_map/while/body/eval_jaxpr/ppermute | solution.py:15
  27.2 0.8 %copy-start.7 = (f32[128]{0:T(128)S(1)}, f32[128]{0:T(128)}, u32[]{:S(2)}) copy-start(f32[128]{0:T(128)} %param.8) | copy-start | bytes 1540
  30.4 2.2 %copy-start = (bf16[128,16,128]{2,0,1:T(8,128)(2,1)}, bf16[128,16,128]{2,0,1:T(8,128)(2,1)S(1)}, u32[]{:S(2)}) copy-start(bf16[128,16,128]{2,0,1:T(8,128)(2,1)S(1)} %copy.116) | copy-start | bytes 1572868
  37.5 0.8 %copy-start.4 = (bf16[1,128,256]{1,2,0:T(8,128)(2,1)S(1)}, bf16[1,128,256]{1,2,0:T(8,128)(2,1)}, u32[]{:S(2)}) copy-start(bf16[1,128,256]{1,2,0:T(8,128)(2,1)} %get-tuple-element.47) | copy-start | bytes 196612
  38.3 2.1 %copy-start.1 = (bf16[128,16,128]{2,0,1:T(8,128)(2,1)S(1)}, bf16[128,16,128]{2,0,1:T(8,128)(2,1)}, u32[]{:S(2)}) copy-start(bf16[128,16,128]{2,0,1:T(8,128)(2,1)} %copy.124) | copy-start | bytes 1572868
  41.4 0.9 %copy-start.3 = (bf16[1,256,256]{1,2,0:T(8,128)(2,1)S(1)}, bf16[1,256,256]{1,2,0:T(8,128)(2,1)}, u32[]{:S(2)}) copy-start(bf16[1,256,256]{1,2,0:T(8,128)(2,1)} %get-tuple-element.45) | copy-start | bytes 393220
  41.4 0.9 %copy-start.5 = (bf16[1,128,256]{1,2,0:T(8,128)(2,1)S(1)}, bf16[1,128,256]{1,2,0:T(8,128)(2,1)}, u32[]{:S(2)}) copy-start(bf16[1,128,256]{1,2,0:T(8,128)(2,1)} %get-tuple-element.47) | copy-start | bytes 196612
  42.3 0.9 %copy-start.2 = (bf16[256,2,128,1]{0,2,1,3:T(8,128)(2,1)S(1)}, bf16[256,2,128,1]{0,2,1,3:T(8,128)(2,1)}, u32[]{:S(2)}) copy-start(bf16[256,2,128,1]{0,2,1,3:T(8,128)(2,1)} %reshape.252) | copy-start | bytes 393220
where the time goes:
time: 51.7 us; the launch traced here: 51 us
  starting transfers between devices  17.5 us (34%)
  local copies, waits for them, and re-layouts  15 us (29%)
  other arithmetic  7.62 us (15%)
  matrix products  5.91 us (11%)
  blocking collectives  4.51 us (9%)
  between operations  0.52 us (1%)
    ppermute x2, starting transfers between devices, shifted(): return lax.ppermute(block, axis, route)  6.16 us
    all_to_all x1, blocking collectives, local(): lax.all_to_all(merged, 'uly', split_axis=0, concat_axis=1, tiled=True)  4.51 us
    all_to_all x1, starting transfers between devices, local(): lax.all_to_all(key_proj, 'uly', split_axis=1, concat_axis=0, tiled=True)  4.04 us
    all_to_all x1, starting transfers between devices, local(): lax.all_to_all(query_proj, 'uly', split_axis=1, concat_axis=0, tiled=True)  3.87 us
    dot_general x4, matrix products, attend(): jnp.einsum('rkgd,nkd->kgrn', query_heads, key_heads, preferred_element_ty...  3.81 us
    all_to_all x1, starting transfers between devices, local(): lax.all_to_all(value_projection, 'uly', split_axis=1, concat_axis=0, tile...  3.4 us
    unnamed x18, local copies, waits for them, and re-layouts  2.43 us
    all_to_all x1, local copies, waits for them, and re-layouts, local(): lax.all_to_all(query_proj, 'uly', split_axis=1, concat_axis=0, tiled=True)  2.31 us
  transfers between devices with their start and end apart: 5, of which 0 were waited for; matrix products, arithmetic and copies ran while one was open for 36% of the time, Pallas kernels for 0%

commit v1 on v0

v1 whole, which is shorter than its diff:
```python
import functools
import math

import jax
import jax.numpy as jnp
import numpy as np
from jax import lax
from jax.experimental import pallas as pl
from jax.experimental.pallas import tpu as pltpu
from jax.sharding import PartitionSpec as P

NEG_FILL = -1e30
ROPE_BASE = 1000000.0
EPSILON = 1e-06
VMEM_LIMIT = 48 * 1024 * 1024


def stretch_device(stretch, cycle):
    return 2 * stretch if stretch < cycle else 2 * (2 * cycle - 1 - stretch) + 1


def forward_route(distance, cycle):
    total = 2 * cycle
    return [
        (stretch_device(s, cycle), stretch_device((s + distance) % total, cycle))
        for s in range(total)
    ]


def rotary_tables(stretches, length, width):
    half = width // 2
    frequency = ROPE_BASE ** (-2.0 * np.arange(half, dtype=np.float64) / width)
    frequency = np.concatenate([frequency, frequency])
    base = (np.arange(stretches, dtype=np.float64) * length)[:, None] * frequency
    offset = np.arange(length, dtype=np.float64)[:, None] * frequency
    sign = np.where(np.arange(width) < half, -1.0, 1.0)
    base = np.concatenate([np.cos(base), np.sin(base)], axis=1)
    offset = np.stack([np.cos(offset), np.sin(offset), np.cos(offset) * sign, np.sin(offset) * sign])
    return base.astype(np.float32), offset.astype(np.float32)


def my_stretch(cycle):
    block = lax.axis_index("blk")
    return jnp.where(lax.axis_index("uly") == 0, block, 2 * cycle - 1 - block)


def gained_tables(base_ref, offset_ref, gain, stretch):
    width = gain.shape[-1]
    base = base_ref[pl.ds(stretch, 1), :]
    base_cos, base_sin = base[:, :width], base[:, width:]
    cosine = base_cos * offset_ref[0] - base_sin * offset_ref[1]
    sine = base_sin * offset_ref[2] + base_cos * offset_ref[3]
    return gain * cosine, pltpu.roll(gain, width // 2, 1) * sine


def rotate_head(raw, cosine, sine):
    values = raw.astype(jnp.float32)
    width = values.shape[-1]
    mean_square = jnp.sum(values * values, axis=-1, keepdims=True) * (1.0 / width)
    turned = values * cosine + pltpu.roll(values, width // 2, 1) * sine
    return (turned * lax.rsqrt(mean_square + EPSILON)).astype(jnp.bfloat16)


def matmul(left, right):
    return jnp.dot(left, right, preferred_element_type=jnp.float32)


def matmul_t(left, right):
    return lax.dot_general(left, right, (((1,), (1,)), ((), ())), preferred_element_type=jnp.float32)


def local_kernel(
    cycle, span, q_ref, k_ref, q_gain_ref, k_gain_ref, base_ref, offset_ref, rotated_ref, score_ref, table_ref
):
    heads, length, width = rotated_ref.shape
    kv_heads = k_ref.shape[1] // width
    group = heads // kv_heads
    stretch = my_stretch(cycle)
    k_gain = k_gain_ref[...]
    q_cos, q_sin = gained_tables(base_ref, offset_ref, q_gain_ref[...], stretch)
    k_cos, k_sin = gained_tables(base_ref, offset_ref, k_gain, stretch)
    for d in range(1, span + 1):
        before = jnp.maximum(stretch - d, 0)
        table_ref[d - 1, 0], table_ref[d - 1, 1] = gained_tables(base_ref, offset_ref, k_gain, before)
    for g in range(kv_heads):
        keys = rotate_head(k_ref[:, g * width : (g + 1) * width], k_cos, k_sin)
        for h in range(g * group, (g + 1) * group):
            rotated_ref[h] = rotate_head(q_ref[:, h * width : (h + 1) * width], q_cos, q_sin)
        queries = rotated_ref[g * group : (g + 1) * group].reshape(group * length, width)
        score_ref[g * group : (g + 1) * group] = matmul_t(queries, keys).reshape(group, length, length)


def weight_kernel(cycle, span, rotated_ref, score_ref, table_ref, *refs):
    key_refs = refs[:span]
    weight_ref, inverse_ref = refs[span:]
    heads, length, width = rotated_ref.shape
    kv_heads = key_refs[0].shape[1] // width
    group = heads // kv_heads
    stretch = my_stretch(cycle)
    to_exponent = math.log2(math.e) / math.sqrt(width)
    rows = lax.broadcasted_iota(jnp.int32, (length, length), 0)
    columns = lax.broadcasted_iota(jnp.int32, (length, length), 1)
    own = columns <= rows
    own_part = own.astype(jnp.float32).astype(jnp.bfloat16)
    far_part = (1.0 - own.astype(jnp.float32)).astype(jnp.bfloat16)
    absent = [jnp.where(stretch >= d, 0.0, NEG_FILL).astype(jnp.float32) for d in range(1, span + 1)]
    for g in range(kv_heads):
        keys = [
            rotate_head(key_refs[d][:, g * width : (g + 1) * width], table_ref[d, 0], table_ref[d, 1])
            for d in range(span)
        ]
        queries = rotated_ref[g * group : (g + 1) * group].reshape(group * length, width)
        far = [matmul_t(queries, keys[d]).reshape(group, length, length) for d in range(span)]
        for i in range(group):
            h = g * group + i
            tiles = [jnp.where(own, score_ref[h], far[span - 1][i] + absent[span - 1])]
            tiles += [far[d][i] + absent[d] for d in range(span - 1)]
            top = functools.reduce(jnp.maximum, tiles)
            top = jnp.max(top, axis=-1, keepdims=True)
            weights = [jnp.exp2((tile - top) * to_exponent) for tile in tiles]
            total = jnp.sum(functools.reduce(jnp.add, weights), axis=-1, keepdims=True)
            inverse_ref[h] = jnp.broadcast_to(1.0 / total, (length, width))
            rounded = [w.astype(jnp.bfloat16) for w in weights]
            weight_ref[h, :, :length] = rounded[0] * own_part
            for d in range(span - 1):
                weight_ref[h, :, (d + 1) * length : (d + 2) * length] = rounded[d + 1]
            weight_ref[h, :, span * length :] = rounded[0] * far_part


def mix_kernel(span, weight_ref, inverse_ref, *refs):
    value_refs = refs[: span + 1]
    out_ref, held_ref, stage_ref, in_sem, out_sem = refs[span + 1 :]
    heads, length, keys = weight_ref.shape
    kv_heads, _, width = held_ref.shape
    group = heads // kv_heads
    fetches = []
    for g in range(kv_heads):
        for d in range(span + 1):
            fetches.append(
                pltpu.make_async_copy(
                    value_refs[d].at[:, g * width : (g + 1) * width],
                    held_ref.at[g, d * length : (d + 1) * length],
                    in_sem.at[g, d],
                )
            )
            fetches[-1].start()
    stores = []
    for g in range(kv_heads):
        for d in range(span + 1):
            fetches[g * (span + 1) + d].wait()
        weights = weight_ref[g * group : (g + 1) * group].reshape(group * length, keys)
        mixed = matmul(weights, held_ref[g]).reshape(group, length, width)
        for i in range(group):
            h = g * group + i
            stage_ref[:, h * width : (h + 1) * width] = (mixed[i] * inverse_ref[h]).astype(jnp.bfloat16)
        block = slice(g * group * width, (g + 1) * group * width)
        stores.append(pltpu.make_async_copy(stage_ref.at[:, block], out_ref.at[:, block], out_sem.at[g]))
        stores[-1].start()
    for store in stores:
        store.wait()


def local(query_proj, key_proj, value_projection, query_gain, key_gain):
    cycle = lax.axis_size("blk")
    span = max(1, cycle // 64)
    length, query_width = query_proj.shape
    width = query_gain.shape[0]
    heads = query_width // width
    kv_heads = key_proj.shape[1] // width
    params = pltpu.CompilerParams(vmem_limit_bytes=VMEM_LIMIT)
    vmem = pl.BlockSpec(memory_space=pltpu.VMEM)
    hbm = pl.BlockSpec(memory_space=pltpu.HBM)

    routes = [forward_route(d, cycle) for d in range(1, span + 1)]
    far_keys = [lax.ppermute(key_proj, ("blk", "uly"), route) for route in routes]
    far_values = [lax.ppermute(value_projection, ("blk", "uly"), route) for route in routes]

    base, offset = rotary_tables(2 * cycle, length, width)
    rotated, scores, tables = pl.pallas_call(
        functools.partial(local_kernel, cycle, span),
        in_specs=[vmem] * 6,
        out_specs=[vmem] * 3,
        out_shape=[
            pltpu.VMEM((heads, length, width), jnp.bfloat16),
            pltpu.VMEM((heads, length, length), jnp.float32),
            pltpu.VMEM((span, 2, length, width), jnp.float32),
        ],
        compiler_params=params,
        name="local_scores",
    )(query_proj, key_proj, query_gain[None], key_gain[None], base, offset)
    weights, inverse = pl.pallas_call(
        functools.partial(weight_kernel, cycle, span),
        in_specs=[vmem] * (3 + span),
        out_specs=[vmem] * 2,
        out_shape=[
            pltpu.VMEM((heads, length, (span + 1) * length), jnp.bfloat16),
            pltpu.VMEM((heads, length, width), jnp.float32),
        ],
        compiler_params=params,
        name="weights",
    )(rotated, scores, tables, *far_keys)
    return pl.pallas_call(
        functools.partial(mix_kernel, span),
        in_specs=[vmem] * 2 + [hbm] * (span + 1),
        out_specs=hbm,
        out_shape=jax.ShapeDtypeStruct(query_proj.shape, jnp.bfloat16),
        scratch_shapes=[
            pltpu.VMEM((kv_heads, (span + 1) * length, width), jnp.bfloat16),
            pltpu.VMEM(query_proj.shape, jnp.bfloat16),
            pltpu.SemaphoreType.DMA((kv_heads, span + 1)),
            pltpu.SemaphoreType.DMA((kv_heads,)),
        ],
        compiler_params=params,
        name="mix_values",
    )(weights, inverse, value_projection, *far_values)


def solution(mesh):
    placed = P(("groups", "blk", "uly"), None)
    return jax.shard_map(
        local,
        mesh=mesh,
        in_specs=(placed, placed, placed, P(), P()),
        out_specs=placed,
        check_vma=False,
    )
```

time: 51.7 us -> 20.9 us (0.40)
  the two profiles are of different devices: /device:TPU:13 before, /device:TPU:0 now
where the time goes in v1:
time: 20.9 us; the launch traced here: 20.6 us
  Pallas kernels  9.62 us (46%)
  local copies, waits for them, and re-layouts  6.44 us (31%)
  starting transfers between devices  4.49 us (21%)
    unnamed x16, local copies, waits for them, and re-layouts  6.44 us
    pallas_call x1, Pallas kernels, local(): pl.pallas_call(functools.partial(weight_kernel, cycle, span), in_specs=[v...  4.57 us
    ppermute x1, starting transfers between devices, local(): lax.ppermute(key_proj, ('blk', 'uly'), route)  2.94 us
    pallas_call x1, Pallas kernels, local(): pl.pallas_call(functools.partial(mix_kernel, span), in_specs=[vmem] * 2 +...  2.56 us
    pallas_call x1, Pallas kernels, local(): pl.pallas_call(functools.partial(local_kernel, cycle, span), in_specs=[vm...  2.5 us
    ppermute x1, starting transfers between devices, local(): lax.ppermute(value_projection, ('blk', 'uly'), route)  1.55 us
  transfers between devices with their start and end apart: 2, of which 0 were waited for; matrix products, arithmetic and copies ran while one was open for 0% of the time, Pallas kernels for 34%

profile of v1, /device:TPU:0, one launch (start us, length us, event | category | flops | bytes accessed | tf_op | source)
XLA Modules:
  0.0 20.6 jit_solution(6879611894752202368)
XLA Ops:
  0.0 2.9 %collective-permute-start = (bf16[128,512]{1,0:T(8,128)(2,1)}, bf16[128,512]{1,0:T(8,128)(2,1)S(1)}, u32[]{:S(2)}, u32[]{:S(2)}) collective-permute-start(bf16[128,512]{1,0:T(8,128)(2,1)} %k_ref.1), channel_id=1, source_target_pairs={{0,2},{2,4},{4,6},{6,8},{8,10},{10,12},{12,14},{14,15},{15,13},{13... | collective-permute-start | bytes 393224 | tf_op jit(solution)/shard_map/ppermute | solution.py:175
  2.9 1.5 %collective-permute-start.1 = (bf16[128,512]{1,0:T(8,128)(2,1)}, bf16[128,512]{1,0:T(8,128)(2,1)S(1)}, u32[]{:S(2)}, u32[]{:S(2)}) collective-permute-start(bf16[128,512]{1,0:T(8,128)(2,1)} %refs_0_.1), channel_id=1, source_target_pairs={{0,2},{2,4},{4,6},{6,8},{8,10},{10,12},{12,14},{14,15},{15,13},{13... | collective-permute-start | bytes 393224 | tf_op jit(solution)/shard_map/ppermute | solution.py:176
  4.5 0.0 copy-start.1
  4.5 1.2 %copy-done.1 = bf16[128,4096]{1,0:T(8,128)(2,1)S(1)} copy-done((bf16[128,4096]{1,0:T(8,128)(2,1)S(1)}, bf16[128,4096]{1,0:T(8,128)(2,1)}, u32[]{:S(2)}) %copy-start.1) | copy-done | bytes 1048600
  5.7 0.0 copy-start.2
  5.7 0.9 %copy-done.2 = f32[4,128,128]{2,1,0:T(8,128)S(1)} copy-done((f32[4,128,128]{2,1,0:T(8,128)S(1)}, f32[4,128,128]{2,1,0:T(8,128)}, u32[]{:S(2)}) %copy-start.2) | copy-done | bytes 262168
  6.7 0.0 copy-start.3
  6.7 0.9 %copy-done.3 = bf16[128,512]{1,0:T(8,128)(2,1)S(1)} copy-done((bf16[128,512]{1,0:T(8,128)(2,1)S(1)}, bf16[128,512]{1,0:T(8,128)(2,1)}, u32[]{:S(2)}) %copy-start.3) | copy-done | bytes 131096
  7.6 0.0 copy-start.5
  7.6 0.7 %copy-done.5 = f32[16,256]{1,0:T(8,128)S(1)} copy-done((f32[16,256]{1,0:T(8,128)S(1)}, f32[16,256]{1,0:T(8,128)}, u32[]{:S(2)}) %copy-start.5) | copy-done | bytes 16408
  8.3 0.0 copy-start.6
  8.3 0.7 %copy-done.6 = f32[128]{0:T(128)S(1)} copy-done((f32[128]{0:T(128)S(1)}, f32[128]{0:T(128)}, u32[]{:S(2)}) %copy-start.6) | copy-done | bytes 536
  8.9 0.0 copy-start.7
  8.9 0.7 %copy-done.7 = f32[128]{0:T(128)S(1)} copy-done((f32[128]{0:T(128)S(1)}, f32[128]{0:T(128)}, u32[]{:S(2)}) %copy-start.7) | copy-done | bytes 536
  9.6 0.0 copy-start.4
  9.6 2.5 %local_scores.1 = (bf16[32,128,128]{2,1,0:T(8,128)(2,1)S(1)}, f32[32,128,128]{2,1,0:T(8,128)S(1)}, f32[1,2,128,128]{3,2,1,0:T(8,128)S(1)}) custom-call(bf16[128,4096]{1,0:T(8,128)(2,1)S(1)} %copy-done.1, bf16[128,512]{1,0:T(8,128)(2,1)S(1)} %copy-done.3, f32[1,128]{1,0:T(1,128)S(1)} %bitcast.2, f32[1,128]{1,0:T(1,128)S(1)} %bitcast.3, ...), custom_call_target="tpu_custom_call" | custom-call | tf_op jit(solution)/shard_map/local_scores/pallas_call | solution.py:179
  12.1 0.0 copy-start
  12.1 1.3 %copy-done = f32[32,128,128]{2,1,0:T(8,128)} copy-done((f32[32,128,128]{2,1,0:T(8,128)}, f32[32,128,128]{2,1,0:T(8,128)S(1)}, u32[]{:S(2)}) %copy-start) | copy-done | bytes 2097176
  13.4 0.0 collective-permute-done.refs_0_
  13.4 4.6 %weights.1 = (bf16[32,128,256]{2,1,0:T(8,128)(2,1)S(1)}, f32[32,128,128]{2,1,0:T(8,128)S(1)}) custom-call(bf16[32,128,128]{2,1,0:T(8,128)(2,1)S(1)} %get-tuple-element.10.rotated_ref, f32[32,128,128]{2,1,0:T(8,128)} %copy-done, f32[1,2,128,128]{3,2,1,0:T(8,128)S(1)} %get-tuple-element.12.table_ref, bf16[128,512]{1,0:T(8,128)(2,1)S(1)} %collective-permute-done.refs_0_), custom_call_target="tpu_custom_call" | custom-call | tf_op jit(solution)/shard_map/weights/pallas_call | solution.py:191
  18.0 0.0 collective-permute-done.1.refs_1_
  18.0 0.0 copy-done.4
  18.0 2.6 %mix_values.1 = bf16[128,4096]{1,0:T(8,128)(2,1)} custom-call(bf16[32,128,256]{2,1,0:T(8,128)(2,1)S(1)} %get-tuple-element.13.weight_ref, f32[32,128,128]{2,1,0:T(8,128)S(1)} %get-tuple-element.14.inverse_ref, bf16[128,512]{1,0:T(8,128)(2,1)S(1)} %copy-done.4, bf16[128,512]{1,0:T(8,128)(2,1)S(1)} %collective-permute-done.1.refs_1_), custom_call_target="tpu_custom_call" | custom-call | tf_op jit(solution)/shard_map/mix_values/pallas_call | solution.py:202
Async XLA Ops:
  0.0 13.4 %collective-permute-start = (bf16[128,512]{1,0:T(8,128)(2,1)}, bf16[128,512]{1,0:T(8,128)(2,1)S(1)}, u32[]{:S(2)}, u32[]{:S(2)}) collective-permute-start(bf16[128,512]{1,0:T(8,128)(2,1)} %k_ref.1), channel_id=1, source_target_pairs={{0,2},{2,4},{4,6},{6,8},{8,10},{10,12},{12,14},{14,15},{15,13},{13... | collective-permute-start | bytes 393224 | tf_op jit(solution)/shard_map/ppermute | solution.py:175
  2.9 15.1 %collective-permute-start.1 = (bf16[128,512]{1,0:T(8,128)(2,1)}, bf16[128,512]{1,0:T(8,128)(2,1)S(1)}, u32[]{:S(2)}, u32[]{:S(2)}) collective-permute-start(bf16[128,512]{1,0:T(8,128)(2,1)} %refs_0_.1), channel_id=1, source_target_pairs={{0,2},{2,4},{4,6},{6,8},{8,10},{10,12},{12,14},{14,15},{15,13},{13... | collective-permute-start | bytes 393224 | tf_op jit(solution)/shard_map/ppermute | solution.py:176
  4.5 1.2 %copy-start.1 = (bf16[128,4096]{1,0:T(8,128)(2,1)S(1)}, bf16[128,4096]{1,0:T(8,128)(2,1)}, u32[]{:S(2)}) copy-start(bf16[128,4096]{1,0:T(8,128)(2,1)} %q_ref.1) | copy-start | bytes 3145732
  5.7 0.9 %copy-start.2 = (f32[4,128,128]{2,1,0:T(8,128)S(1)}, f32[4,128,128]{2,1,0:T(8,128)}, u32[]{:S(2)}) copy-start(f32[4,128,128]{2,1,0:T(8,128)} %constant.5.clone.offset_ref) | copy-start | bytes 786436
  6.7 0.9 %copy-start.3 = (bf16[128,512]{1,0:T(8,128)(2,1)S(1)}, bf16[128,512]{1,0:T(8,128)(2,1)}, u32[]{:S(2)}) copy-start(bf16[128,512]{1,0:T(8,128)(2,1)} %k_ref.1) | copy-start | bytes 393220
  7.6 0.7 %copy-start.5 = (f32[16,256]{1,0:T(8,128)S(1)}, f32[16,256]{1,0:T(8,128)}, u32[]{:S(2)}) copy-start(f32[16,256]{1,0:T(8,128)} %constant.4.clone.base_ref) | copy-start | bytes 49156
  8.3 0.7 %copy-start.6 = (f32[128]{0:T(128)S(1)}, f32[128]{0:T(128)}, u32[]{:S(2)}) copy-start(f32[128]{0:T(128)} %param.10) | copy-start | bytes 1540
  8.9 0.7 %copy-start.7 = (f32[128]{0:T(128)S(1)}, f32[128]{0:T(128)}, u32[]{:S(2)}) copy-start(f32[128]{0:T(128)} %param.11) | copy-start | bytes 1540
  9.6 8.4 %copy-start.4 = (bf16[128,512]{1,0:T(8,128)(2,1)S(1)}, bf16[128,512]{1,0:T(8,128)(2,1)}, u32[]{:S(2)}) copy-start(bf16[128,512]{1,0:T(8,128)(2,1)} %refs_0_.1) | copy-start | bytes 393220
  12.1 1.3 %copy-start = (f32[32,128,128]{2,1,0:T(8,128)}, f32[32,128,128]{2,1,0:T(8,128)S(1)}, u32[]{:S(2)}) copy-start(f32[32,128,128]{2,1,0:T(8,128)S(1)} %get-tuple-element.11.score_ref) | copy-start | bytes 6291460

commit v2 on v1

v2 whole, which is shorter than its diff:
```python
import functools
import math

import jax
import jax.numpy as jnp
import numpy as np
from jax import lax
from jax.experimental import pallas as pl
from jax.experimental.pallas import tpu as pltpu
from jax.sharding import PartitionSpec as P

NEG_FILL = -1e30
ROPE_BASE = 1000000.0
EPSILON = 1e-06
VMEM_LIMIT = 16 * 1024 * 1024


def stretch_device(stretch, cycle):
    return 2 * stretch if stretch < cycle else 2 * (2 * cycle - 1 - stretch) + 1


def forward_route(distance, cycle):
    total = 2 * cycle
    return [
        (stretch_device(s, cycle), stretch_device((s + distance) % total, cycle))
        for s in range(total)
    ]


def rotary_tables(stretches, length, width):
    half = width // 2
    frequency = ROPE_BASE ** (-2.0 * np.arange(half, dtype=np.float64) / width)
    frequency = np.concatenate([frequency, frequency])
    base = (np.arange(stretches, dtype=np.float64) * length)[:, None] * frequency
    offset = np.arange(length, dtype=np.float64)[:, None] * frequency
    sign = np.where(np.arange(width) < half, -1.0, 1.0)
    base = np.concatenate([np.cos(base), np.sin(base)], axis=1)
    offset = np.stack([np.cos(offset), np.sin(offset), np.cos(offset) * sign, np.sin(offset) * sign])
    return base.astype(np.float32), offset.astype(np.float32)


def my_stretch(cycle):
    block = lax.axis_index("blk")
    return jnp.where(lax.axis_index("uly") == 0, block, 2 * cycle - 1 - block)


def gained_tables(base_ref, offset_ref, gain, stretch):
    width = gain.shape[-1]
    base = base_ref[pl.ds(stretch, 1), :]
    base_cos, base_sin = base[:, :width], base[:, width:]
    cosine = base_cos * offset_ref[0] - base_sin * offset_ref[1]
    sine = base_sin * offset_ref[2] + base_cos * offset_ref[3]
    return gain * cosine, pltpu.roll(gain, width // 2, 1) * sine


def rotate_head(raw, cosine, sine):
    values = raw.astype(jnp.float32)
    width = values.shape[-1]
    mean_square = jnp.sum(values * values, axis=-1, keepdims=True) * (1.0 / width)
    turned = values * cosine + pltpu.roll(values, width // 2, 1) * sine
    return (turned * lax.rsqrt(mean_square + EPSILON)).astype(jnp.bfloat16)


def matmul(left, right):
    return jnp.dot(left, right, preferred_element_type=jnp.float32)


def matmul_t(left, right):
    return lax.dot_general(left, right, (((1,), (1,)), ((), ())), preferred_element_type=jnp.float32)


def local_kernel(
    cycle,
    span,
    q_hbm,
    k_hbm,
    v_hbm,
    q_gain_hbm,
    k_gain_hbm,
    base_hbm,
    offset_hbm,
    rotated_ref,
    score_ref,
    table_ref,
    value_ref,
    q_ref,
    k_ref,
    q_gain_ref,
    k_gain_ref,
    base_ref,
    offset_ref,
    small_sem,
    q_sem,
    v_sem,
):
    heads, length, width = rotated_ref.shape
    kv_heads = k_ref.shape[1] // width
    group = heads // kv_heads
    stretch = my_stretch(cycle)
    smalls = [
        pltpu.make_async_copy(source, target, small_sem.at[i])
        for i, (source, target) in enumerate(
            [
                (q_gain_hbm, q_gain_ref),
                (k_gain_hbm, k_gain_ref),
                (base_hbm, base_ref),
                (offset_hbm, offset_ref),
                (k_hbm, k_ref),
            ]
        )
    ]
    for copy in smalls:
        copy.start()
    q_copies = []
    for g in range(kv_heads):
        block = slice(g * group * width, (g + 1) * group * width)
        q_copies.append(pltpu.make_async_copy(q_hbm.at[:, block], q_ref.at[:, block], q_sem.at[g]))
        q_copies[-1].start()
    v_copy = pltpu.make_async_copy(v_hbm, value_ref, v_sem)
    v_copy.start()
    for copy in smalls:
        copy.wait()

    k_gain = k_gain_ref[...]
    q_cos, q_sin = gained_tables(base_ref, offset_ref, q_gain_ref[...], stretch)
    k_cos, k_sin = gained_tables(base_ref, offset_ref, k_gain, stretch)
    for d in range(1, span + 1):
        before = jnp.maximum(stretch - d, 0)
        table_ref[d - 1, 0], table_ref[d - 1, 1] = gained_tables(base_ref, offset_ref, k_gain, before)
    rows = lax.broadcasted_iota(jnp.int32, (length, length), 0)
    columns = lax.broadcasted_iota(jnp.int32, (length, length), 1)
    own = columns <= rows
    for g in range(kv_heads):
        keys = rotate_head(k_ref[:, g * width : (g + 1) * width], k_cos, k_sin)
        q_copies[g].wait()
        for h in range(g * group, (g + 1) * group):
            rotated_ref[h] = rotate_head(q_ref[:, h * width : (h + 1) * width], q_cos, q_sin)
        queries = rotated_ref[g * group : (g + 1) * group].reshape(group * length, width)
        scores = matmul_t(queries, keys).reshape(group, length, length)
        for i in range(group):
            score_ref[g * group + i] = jnp.where(own, scores[i], NEG_FILL)
    v_copy.wait()


def weight_kernel(cycle, span, rotated_ref, score_ref, table_ref, *refs):
    key_refs = refs[:span]
    weight_ref = refs[span]
    heads, length, width = rotated_ref.shape
    kv_heads = key_refs[0].shape[1] // width
    group = heads // kv_heads
    stretch = my_stretch(cycle)
    to_exponent = math.log2(math.e) / math.sqrt(width)
    rows = lax.broadcasted_iota(jnp.int32, (length, length), 0)
    columns = lax.broadcasted_iota(jnp.int32, (length, length), 1)
    own = columns <= rows
    near = columns <= jnp.where(stretch >= span, rows, length)
    for g in range(kv_heads):
        keys = [
            rotate_head(key_refs[d][:, g * width : (g + 1) * width], table_ref[d, 0], table_ref[d, 1])
            for d in range(span)
        ]
        queries = rotated_ref[g * group : (g + 1) * group].reshape(group * length, width)
        far = [matmul_t(queries, keys[d]).reshape(group, length, length) for d in range(span)]
        for i in range(group):
            h = g * group + i
            tiles = [jnp.where(near, score_ref[h], far[span - 1][i])]
            for d in range(span - 1):
                tiles.append(jnp.where(stretch > d, far[d][i], NEG_FILL))
            top = jnp.max(functools.reduce(jnp.maximum, tiles), axis=-1, keepdims=True)
            weights = [jnp.exp2((tile - top) * to_exponent) for tile in tiles]
            weight_ref[h, :, :length] = jnp.where(own, weights[0], 0.0).astype(jnp.bfloat16)
            for d in range(span - 1):
                weight_ref[h, :, (d + 1) * length : (d + 2) * length] = weights[d + 1].astype(jnp.bfloat16)
            weight_ref[h, :, span * length :] = jnp.where(own, 0.0, weights[0]).astype(jnp.bfloat16)


def mix_kernel(parts, weight_ref, *refs):
    out_hbm, stage_ref, out_sem = refs[-3:]
    value_refs = refs[:-3]
    heads, length, keys = weight_ref.shape
    width = stage_ref.shape[1] // heads
    kv_heads = value_refs[0].shape[1] // width
    group = heads // kv_heads
    step = group // parts
    ones = jnp.ones((keys, width), jnp.bfloat16)
    stores = []
    for g in range(kv_heads):
        values = jnp.concatenate([ref[:, g * width : (g + 1) * width] for ref in value_refs], axis=0)
        values = jnp.concatenate([values, ones], axis=1)
        for first in range(g * group, (g + 1) * group, step):
            weights = weight_ref[first : first + step].reshape(step * length, keys)
            mixed = matmul(weights, values)
            mixed = mixed[:, :width] * (1.0 / mixed[:, width:])
            for i in range(step):
                h = first + i
                stage_ref[:, h * width : (h + 1) * width] = mixed[i * length : (i + 1) * length].astype(jnp.bfloat16)
            block = slice(first * width, (first + step) * width)
            stores.append(
                pltpu.make_async_copy(stage_ref.at[:, block], out_hbm.at[:, block], out_sem.at[first // step])
            )
            stores[-1].start()
    for store in stores:
        store.wait()


def local(query_proj, key_proj, value_projection, query_gain, key_gain):
    cycle = lax.axis_size("blk")
    span = max(1, cycle // 64)
    length, query_width = query_proj.shape
    kv_width = key_proj.shape[1]
    width = query_gain.shape[0]
    heads = query_width // width
    kv_heads = kv_width // width
    params = pltpu.CompilerParams(vmem_limit_bytes=VMEM_LIMIT)
    vmem = pl.BlockSpec(memory_space=pltpu.VMEM)
    hbm = pl.BlockSpec(memory_space=pltpu.HBM)

    routes = [forward_route(d, cycle) for d in range(1, span + 1)]
    far_keys = [lax.ppermute(key_proj, ("blk", "uly"), route) for route in routes]
    far_values = [lax.ppermute(value_projection, ("blk", "uly"), route) for route in routes]

    base, offset = rotary_tables(2 * cycle, length, width)
    operands = (query_proj, key_proj, value_projection, query_gain[None], key_gain[None], base, offset)
    rotated, scores, tables, values = pl.pallas_call(
        functools.partial(local_kernel, cycle, span),
        in_specs=[hbm] * 7,
        out_specs=[vmem] * 4,
        out_shape=[
            pltpu.VMEM((heads, length, width), jnp.bfloat16),
            pltpu.VMEM((heads, length, length), jnp.float32),
            pltpu.VMEM((span, 2, length, width), jnp.float32),
            pltpu.VMEM((length, kv_width), jnp.bfloat16),
        ],
        scratch_shapes=[
            pltpu.VMEM((length, query_width), jnp.bfloat16),
            pltpu.VMEM((length, kv_width), jnp.bfloat16),
            pltpu.VMEM((1, width), jnp.float32),
            pltpu.VMEM((1, width), jnp.float32),
            pltpu.VMEM(base.shape, jnp.float32),
            pltpu.VMEM(offset.shape, jnp.float32),
            pltpu.SemaphoreType.DMA((5,)),
            pltpu.SemaphoreType.DMA((kv_heads,)),
            pltpu.SemaphoreType.DMA,
        ],
        compiler_params=params,
        name="local_scores",
    )(*[pltpu.with_memory_space_constraint(x, pltpu.HBM) for x in operands])
    weights = pl.pallas_call(
        functools.partial(weight_kernel, cycle, span),
        in_specs=[vmem] * (3 + span),
        out_specs=vmem,
        out_shape=pltpu.VMEM((heads, length, (span + 1) * length), jnp.bfloat16),
        compiler_params=params,
        name="weights",
    )(rotated, scores, tables, *far_keys)
    parts = 2 if heads // kv_heads % 2 == 0 else 1
    return pl.pallas_call(
        functools.partial(mix_kernel, parts),
        in_specs=[vmem] * (2 + span),
        out_specs=hbm,
        out_shape=jax.ShapeDtypeStruct(query_proj.shape, jnp.bfloat16),
        scratch_shapes=[
            pltpu.VMEM(query_proj.shape, jnp.bfloat16),
            pltpu.SemaphoreType.DMA((kv_heads * parts,)),
        ],
        compiler_params=params,
        name="mix_values",
    )(weights, values, *far_values)


def solution(mesh):
    placed = P(("groups", "blk", "uly"), None)
    return jax.shard_map(
        local,
        mesh=mesh,
        in_specs=(placed, placed, placed, P(), P()),
        out_specs=placed,
        check_vma=False,
    )
```

time: 20.9 us -> 12.6 us (0.60)
  local copies, waits for them, and re-layouts: 6.44 us -> 0 us
  Pallas kernels: 9.62 us -> 7.94 us
    unnamed x16 -> x0, local copies, waits for them, and re-layouts: 6.44 us -> none
    pallas_call x1, Pallas kernels: 4.57 us -> 1.35 us  [local(): pl.pallas_call(functools.partial(weight_kernel, cycle, span), in_specs=[v...]
    pallas_call x2, Pallas kernels: 5.05 us -> 6.59 us  [the longest x1 5.04 us: local(): pl.pallas_call(functools.partial(local_kernel, cycle, span), in_specs=[hb...]
  transfers between devices with their start and end apart: 2 -> 2, of which waited for: 0 -> 0; matrix products, arithmetic and copies ran while one was open for 0% -> 0% of each run, Pallas kernels for 34% -> 51%
where the time goes in v2:
time: 12.6 us; the launch traced here: 12.5 us
  Pallas kernels  7.94 us (63%)
  starting transfers between devices  4.49 us (36%)
    pallas_call x1, Pallas kernels, local(): pl.pallas_call(functools.partial(local_kernel, cycle, span), in_specs=[hb...  5.04 us
    ppermute x1, starting transfers between devices, local(): lax.ppermute(key_proj, ('blk', 'uly'), route)  2.94 us
    pallas_call x1, Pallas kernels, local(): pl.pallas_call(functools.partial(mix_kernel, parts), in_specs=[vmem] * (2...  1.55 us
    ppermute x1, starting transfers between devices, local(): lax.ppermute(value_projection, ('blk', 'uly'), route)  1.55 us
    pallas_call x1, Pallas kernels, local(): pl.pallas_call(functools.partial(weight_kernel, cycle, span), in_specs=[v...  1.35 us
  transfers between devices with their start and end apart: 2, of which 0 were waited for; matrix products, arithmetic and copies ran while one was open for 0% of the time, Pallas kernels for 51%

profile of v2, /device:TPU:0, one launch (start us, length us, event | category | flops | bytes accessed | tf_op | source)
XLA Modules:
  0.0 12.5 jit_solution(5870938156007624817)
XLA Ops:
  0.0 2.9 %collective-permute-start = (bf16[128,512]{1,0:T(8,128)(2,1)}, bf16[128,512]{1,0:T(8,128)(2,1)S(1)}, u32[]{:S(2)}, u32[]{:S(2)}) collective-permute-start(bf16[128,512]{1,0:T(8,128)(2,1)} %k_hbm.1), channel_id=1, source_target_pairs={{0,2},{2,4},{4,6},{6,8},{8,10},{10,12},{12,14},{14,15},{15,13},{13... | collective-permute-start | bytes 393224 | tf_op jit(solution)/shard_map/ppermute | solution.py:219
  2.9 1.5 %collective-permute-start.1 = (bf16[128,512]{1,0:T(8,128)(2,1)}, bf16[128,512]{1,0:T(8,128)(2,1)S(1)}, u32[]{:S(2)}, u32[]{:S(2)}) collective-permute-start(bf16[128,512]{1,0:T(8,128)(2,1)} %v_hbm.1), channel_id=1, source_target_pairs={{0,2},{2,4},{4,6},{6,8},{8,10},{10,12},{12,14},{14,15},{15,13},{13... | collective-permute-start | bytes 393224 | tf_op jit(solution)/shard_map/ppermute | solution.py:220
  4.5 5.0 %local_scores.1 = (bf16[32,128,128]{2,1,0:T(8,128)(2,1)S(1)}, f32[32,128,128]{2,1,0:T(8,128)S(1)}, f32[1,2,128,128]{3,2,1,0:T(8,128)S(1)}, bf16[128,512]{1,0:T(8,128)(2,1)S(1)}) custom-call(bf16[128,4096]{1,0:T(8,128)(2,1)} %q_hbm.1, bf16[128,512]{1,0:T(8,128)(2,1)} %k_hbm.1, bf16[128,512]{1,0:T(8,128)(2,1)} %v_hbm.1, f32[1,128]{1,0:T(1,128)} %bitcast.2, ...), custom_call_target="tpu_custom_call" | custom-call | tf_op jit(solution)/shard_map/local_scores/pallas_call | solution.py:224
  9.5 0.0 collective-permute-done.refs_0_
  9.5 1.4 %weights.1.weight_ref = bf16[32,128,256]{2,1,0:T(8,128)(2,1)S(1)} custom-call(bf16[32,128,128]{2,1,0:T(8,128)(2,1)S(1)} %get-tuple-element.9.rotated_ref, f32[32,128,128]{2,1,0:T(8,128)S(1)} %get-tuple-element.10.score_ref, f32[1,2,128,128]{3,2,1,0:T(8,128)S(1)} %get-tuple-element.11.table_ref, bf16[128,512]{1,0:T(8,128)(2,1)S(1)} %collective-permute-done.refs_0_), custom_call_target="tpu_custom_call" | custom-call | tf_op jit(solution)/shard_map/weights/pallas_call | solution.py:248
  10.9 0.0 collective-permute-done.1.refs_1_
  10.9 1.6 %mix_values.1 = bf16[128,4096]{1,0:T(8,128)(2,1)} custom-call(bf16[32,128,256]{2,1,0:T(8,128)(2,1)S(1)} %weights.1.weight_ref, bf16[128,512]{1,0:T(8,128)(2,1)S(1)} %get-tuple-element.12.refs_0_, bf16[128,512]{1,0:T(8,128)(2,1)S(1)} %collective-permute-done.1.refs_1_), custom_call_target="tpu_custom_call" | custom-call | tf_op jit(solution)/shard_map/mix_values/pallas_call | solution.py:257
Async XLA Ops:
  0.0 9.5 %collective-permute-start = (bf16[128,512]{1,0:T(8,128)(2,1)}, bf16[128,512]{1,0:T(8,128)(2,1)S(1)}, u32[]{:S(2)}, u32[]{:S(2)}) collective-permute-start(bf16[128,512]{1,0:T(8,128)(2,1)} %k_hbm.1), channel_id=1, source_target_pairs={{0,2},{2,4},{4,6},{6,8},{8,10},{10,12},{12,14},{14,15},{15,13},{13... | collective-permute-start | bytes 393224 | tf_op jit(solution)/shard_map/ppermute | solution.py:219
  2.9 8.0 %collective-permute-start.1 = (bf16[128,512]{1,0:T(8,128)(2,1)}, bf16[128,512]{1,0:T(8,128)(2,1)S(1)}, u32[]{:S(2)}, u32[]{:S(2)}) collective-permute-start(bf16[128,512]{1,0:T(8,128)(2,1)} %v_hbm.1), channel_id=1, source_target_pairs={{0,2},{2,4},{4,6},{6,8},{8,10},{10,12},{12,14},{14,15},{15,13},{13... | collective-permute-start | bytes 393224 | tf_op jit(solution)/shard_map/ppermute | solution.py:220

commit v3 on v2

v3 whole, which is shorter than its diff:
```python
import functools
import math

import jax
import jax.numpy as jnp
import numpy as np
from jax import lax
from jax.experimental import pallas as pl
from jax.experimental.pallas import tpu as pltpu
from jax.sharding import PartitionSpec as P

NEG_FILL = -1e30
ROPE_BASE = 1000000.0
EPSILON = 1e-06
DOT_HEADS = 4
LOOP_A, LOOP_B, LOOP_C = False, False, False
VMEM_LIMIT = 16 * 1024 * 1024


def stretch_device(stretch, cycle):
    return 2 * stretch if stretch < cycle else 2 * (2 * cycle - 1 - stretch) + 1


def forward_route(distance, cycle):
    total = 2 * cycle
    return [
        (stretch_device(s, cycle), stretch_device((s + distance) % total, cycle))
        for s in range(total)
    ]


def rotary_tables(stretches, span, length, width):
    half = width // 2
    frequency = ROPE_BASE ** (-2.0 * np.arange(half, dtype=np.float64) / width)
    before = np.maximum(np.arange(stretches)[:, None] - np.arange(span + 1), 0).astype(np.float64)
    base = (before * length)[:, :, None] * frequency
    offset = np.arange(length, dtype=np.float64)[:, None] * frequency
    base = np.concatenate([np.cos(base), np.sin(base)], axis=-1)
    offset = np.concatenate([np.cos(offset), np.sin(offset)], axis=-1)
    return base.astype(np.float32), offset.astype(np.float32)


def my_stretch(cycle):
    block = lax.axis_index("blk")
    return jnp.where(lax.axis_index("uly") == 0, block, 2 * cycle - 1 - block)


def spread(packed):
    half = packed.shape[-1] // 2
    first = lax.broadcasted_iota(jnp.int32, packed.shape, 1) < half
    turned = pltpu.roll(packed, half, 1)
    return jnp.where(first, packed, turned), jnp.where(first, turned, packed)


def gained_tables(base, offset, gain):
    width = gain.shape[-1]
    half = width // 2
    gain = gain * math.sqrt(width)
    turned_gain = pltpu.roll(gain, half, 1)
    turned_gain = jnp.where(lax.broadcasted_iota(jnp.int32, gain.shape, 1) < half, -turned_gain, turned_gain)
    (base_cos, base_sin), (cosine, sine) = base, offset
    return gain * (base_cos * cosine - base_sin * sine), turned_gain * (base_sin * cosine + base_cos * sine)


def rotate_head(raw, cosine, sine):
    values = raw.astype(jnp.float32)
    width = values.shape[-1]
    square_sum = jnp.sum(values * values, axis=-1, keepdims=True)
    turned = values * cosine + pltpu.roll(values, width // 2, 1) * sine
    return (turned * lax.rsqrt(square_sum + width * EPSILON)).astype(jnp.bfloat16)


def columns_of(block, width):
    if isinstance(block, int):
        return slice(block * width, (block + 1) * width)
    return pl.ds(pl.multiple_of(block * width, width), width)


def loop(rolled, count, body):
    if rolled:
        lax.fori_loop(0, count, body, None)
    else:
        for g in range(count):
            body(g, None)


def matmul(left, right):
    return jnp.dot(left, right, preferred_element_type=jnp.float32)


def matmul_t(left, right):
    return lax.dot_general(left, right, (((1,), (1,)), ((), ())), preferred_element_type=jnp.float32)


def local_kernel(
    cycle,
    span,
    q_hbm,
    k_hbm,
    v_hbm,
    q_gain_hbm,
    k_gain_hbm,
    base_hbm,
    offset_hbm,
    rotated_ref,
    score_ref,
    table_ref,
    value_ref,
    q_ref,
    k_ref,
    q_gain_ref,
    k_gain_ref,
    base_ref,
    offset_ref,
    small_sem,
    q_sem,
    v_sem,
):
    heads, length, width = rotated_ref.shape
    kv_heads = k_ref.shape[1] // width
    group = heads // kv_heads
    stretch = my_stretch(cycle)
    smalls = [
        pltpu.make_async_copy(source, target, small_sem.at[i])
        for i, (source, target) in enumerate(
            [
                (q_gain_hbm, q_gain_ref),
                (k_gain_hbm, k_gain_ref),
                (base_hbm.at[stretch], base_ref),
                (offset_hbm, offset_ref),
                (k_hbm, k_ref),
            ]
        )
    ]
    for copy in smalls:
        copy.start()

    def q_copy(g):
        return pltpu.make_async_copy(q_hbm.at[:, columns_of(g, group * width)], q_ref.at[g], q_sem.at[g])

    for g in range(kv_heads):
        q_copy(g).start()
    v_copy = pltpu.make_async_copy(v_hbm, value_ref, v_sem)
    v_copy.start()
    for copy in smalls:
        copy.wait()

    k_gain = k_gain_ref[...]
    bases = [spread(base_ref[d : d + 1]) for d in range(span + 1)]
    offset = spread(offset_ref[...])
    q_cos, q_sin = gained_tables(bases[0], offset, q_gain_ref[...])
    k_cos, k_sin = gained_tables(bases[0], offset, k_gain)
    for d in range(span):
        table_ref[d, 0], table_ref[d, 1] = gained_tables(bases[d + 1], offset, k_gain)
    rows = lax.broadcasted_iota(jnp.int32, (length, length), 0)
    columns = lax.broadcasted_iota(jnp.int32, (length, length), 1)
    own = columns <= rows
    keys = [rotate_head(k_ref[:, columns_of(g, width)], k_cos, k_sin) for g in range(kv_heads)]

    def score(g):
        for i in range(group):
            scores = matmul_t(rotated_ref[g * group + i], keys[g])
            score_ref[g * group + i] = jnp.where(own, scores, NEG_FILL)

    for g in range(kv_heads):
        q_copy(g).wait()
        for i in range(group):
            rotated_ref[g * group + i] = rotate_head(q_ref[g, :, i * width : (i + 1) * width], q_cos, q_sin)
        if g > 0:
            score(g - 1)
    score(kv_heads - 1)
    v_copy.wait()


def weight_kernel(cycle, span, rotated_ref, score_ref, table_ref, *refs):
    key_refs = refs[:span]
    weight_ref = refs[span]
    heads, length, width = rotated_ref.shape
    kv_heads = key_refs[0].shape[1] // width
    group = heads // kv_heads
    stretch = my_stretch(cycle)
    to_exponent = math.log2(math.e) / math.sqrt(width)
    rows = lax.broadcasted_iota(jnp.int32, (length, length), 0)
    columns = lax.broadcasted_iota(jnp.int32, (length, length), 1)
    own = columns <= rows
    near = columns <= jnp.where(stretch >= span, rows, length)

    def one_group(g, carry):
        keys = [
            rotate_head(key_refs[d][:, columns_of(g, width)], table_ref[d, 0], table_ref[d, 1]) for d in range(span)
        ]
        for i in range(group):
            h = g * group + i
            far = [matmul_t(rotated_ref[h], keys[d]) for d in range(span)]
            tiles = [jnp.where(near, score_ref[h], far[span - 1])]
            for d in range(span - 1):
                tiles.append(jnp.where(stretch > d, far[d], NEG_FILL))
            top = jnp.max(functools.reduce(jnp.maximum, tiles), axis=-1, keepdims=True)
            weights = [jnp.exp2((tile - top) * to_exponent) for tile in tiles]
            weights = [jnp.where(own, weights[0], 0.0), *weights[1:], jnp.where(own, 0.0, weights[0])]
            weight_ref[h] = jnp.concatenate(weights, axis=1).astype(jnp.bfloat16)
        return carry

    loop(LOOP_B, kv_heads, one_group)


def mix_kernel(weight_ref, *refs):
    out_hbm, stage_ref, out_sem = refs[-3:]
    value_refs = refs[:-3]
    heads, length, keys = weight_ref.shape
    kv_heads, _, group_width = stage_ref.shape
    group = heads // kv_heads
    width = group_width // group
    ones = jnp.ones((keys, width), jnp.bfloat16)

    def store(g):
        return pltpu.make_async_copy(stage_ref.at[g], out_hbm.at[:, columns_of(g, group_width)], out_sem.at[g])

    def one_group(g, carry):
        values = jnp.concatenate([ref[:, columns_of(g, width)] for ref in value_refs], axis=0)
        values = jnp.concatenate([values, ones], axis=1)
        for first in range(0, group, DOT_HEADS):
            weights = weight_ref[g * group + first : g * group + first + DOT_HEADS]
            mixed = matmul(weights.reshape(DOT_HEADS * length, keys), values)
            mixed = mixed[:, :width] * (1.0 / mixed[:, width:])
            for i in range(DOT_HEADS):
                stage_ref[g, :, columns_of(first + i, width)] = mixed[i * length : (i + 1) * length].astype(jnp.bfloat16)
        store(g).start()
        return carry

    loop(LOOP_C, kv_heads, one_group)
    for g in range(kv_heads):
        store(g).wait()


def local(query_proj, key_proj, value_projection, query_gain, key_gain):
    cycle = lax.axis_size("blk")
    span = max(1, cycle // 64)
    length, query_width = query_proj.shape
    kv_width = key_proj.shape[1]
    width = query_gain.shape[0]
    heads = query_width // width
    kv_heads = kv_width // width
    params = pltpu.CompilerParams(vmem_limit_bytes=VMEM_LIMIT)
    vmem = pl.BlockSpec(memory_space=pltpu.VMEM)
    hbm = pl.BlockSpec(memory_space=pltpu.HBM)

    routes = [forward_route(d, cycle) for d in range(1, span + 1)]
    far_keys = [lax.ppermute(key_proj, ("blk", "uly"), route) for route in routes]
    far_values = [lax.ppermute(value_projection, ("blk", "uly"), route) for route in routes]

    base, offset = rotary_tables(2 * cycle, span, length, width)
    operands = (query_proj, key_proj, value_projection, query_gain[None], key_gain[None], base, offset)
    rotated, scores, tables, values = pl.pallas_call(
        functools.partial(local_kernel, cycle, span),
        in_specs=[hbm] * 7,
        out_specs=[vmem] * 4,
        out_shape=[
            pltpu.VMEM((heads, length, width), jnp.bfloat16),
            pltpu.VMEM((heads, length, length), jnp.float32),
            pltpu.VMEM((span, 2, length, width), jnp.float32),
            pltpu.VMEM((length, kv_width), jnp.bfloat16),
        ],
        scratch_shapes=[
            pltpu.VMEM((kv_heads, length, query_width // kv_heads), jnp.bfloat16),
            pltpu.VMEM((length, kv_width), jnp.bfloat16),
            pltpu.VMEM((1, width), jnp.float32),
            pltpu.VMEM((1, width), jnp.float32),
            pltpu.VMEM(base.shape[1:], jnp.float32),
            pltpu.VMEM(offset.shape, jnp.float32),
            pltpu.SemaphoreType.DMA((5,)),
            pltpu.SemaphoreType.DMA((kv_heads,)),
            pltpu.SemaphoreType.DMA,
        ],
        compiler_params=params,
        name="local_scores",
    )(*[pltpu.with_memory_space_constraint(x, pltpu.HBM) for x in operands])
    weights = pl.pallas_call(
        functools.partial(weight_kernel, cycle, span),
        in_specs=[vmem] * (3 + span),
        out_specs=vmem,
        out_shape=pltpu.VMEM((heads, length, (span + 1) * length), jnp.bfloat16),
        compiler_params=params,
        name="weights",
    )(rotated, scores, tables, *far_keys)
    return pl.pallas_call(
        mix_kernel,
        in_specs=[vmem] * (2 + span),
        out_specs=hbm,
        out_shape=jax.ShapeDtypeStruct(query_proj.shape, jnp.bfloat16),
        scratch_shapes=[
            pltpu.VMEM((kv_heads, length, query_width // kv_heads), jnp.bfloat16),
            pltpu.SemaphoreType.DMA((kv_heads,)),
        ],
        compiler_params=params,
        name="mix_values",
    )(weights, values, *far_values)


def solution(mesh):
    placed = P(("groups", "blk", "uly"), None)
    return jax.shard_map(
        local,
        mesh=mesh,
        in_specs=(placed, placed, placed, P(), P()),
        out_specs=placed,
        check_vma=False,
    )
```

time: 12.6 us -> 11.3 us (0.90)
  Pallas kernels: 7.94 us -> 6.57 us
    pallas_call x1, Pallas kernels: 5.04 us -> 3.86 us  [local(): pl.pallas_call(functools.partial(local_kernel, cycle, span), in_specs=[hb...]
  transfers between devices with their start and end apart: 2 -> 2, of which waited for: 0 -> 1; matrix products, arithmetic and copies ran while one was open for 0% -> 0% of each run, Pallas kernels for 51% -> 46%
where the time goes in v3:
time: 11.3 us; the launch traced here: 11.2 us
  Pallas kernels  6.57 us (58%)
  starting transfers between devices  4.49 us (40%)
    pallas_call x1, Pallas kernels, local(): pl.pallas_call(functools.partial(local_kernel, cycle, span), in_specs=[hb...  3.86 us
    ppermute x1, starting transfers between devices, local(): lax.ppermute(key_proj, ('blk', 'uly'), route)  2.94 us
    ppermute x1, starting transfers between devices, local(): lax.ppermute(value_projection, ('blk', 'uly'), route)  1.55 us
    pallas_call x1, Pallas kernels, local(): pl.pallas_call(mix_kernel, in_specs=[vmem] * (2 + span), out_specs=hbm, o...  1.46 us
    pallas_call x1, Pallas kernels, local(): pl.pallas_call(functools.partial(weight_kernel, cycle, span), in_specs=[v...  1.25 us
  transfers between devices with their start and end apart: 2, of which 1 were waited for; matrix products, arithmetic and copies ran while one was open for 0% of the time, Pallas kernels for 46%

profile of v3, /device:TPU:0, one launch (start us, length us, event | category | flops | bytes accessed | tf_op | source)
XLA Modules:
  0.0 11.2 jit_solution(8686422288667200854)
XLA Ops:
  0.0 2.9 %collective-permute-start = (bf16[128,512]{1,0:T(8,128)(2,1)}, bf16[128,512]{1,0:T(8,128)(2,1)S(1)}, u32[]{:S(2)}, u32[]{:S(2)}) collective-permute-start(bf16[128,512]{1,0:T(8,128)(2,1)} %k_hbm.1), channel_id=1, source_target_pairs={{0,2},{2,4},{4,6},{6,8},{8,10},{10,12},{12,14},{14,15},{15,13},{13... | collective-permute-start | bytes 393224 | tf_op jit(solution)/shard_map/ppermute | solution.py:249
  2.9 1.5 %collective-permute-start.1 = (bf16[128,512]{1,0:T(8,128)(2,1)}, bf16[128,512]{1,0:T(8,128)(2,1)S(1)}, u32[]{:S(2)}, u32[]{:S(2)}) collective-permute-start(bf16[128,512]{1,0:T(8,128)(2,1)} %v_hbm.1), channel_id=1, source_target_pairs={{0,2},{2,4},{4,6},{6,8},{8,10},{10,12},{12,14},{14,15},{15,13},{13... | collective-permute-start | bytes 393224 | tf_op jit(solution)/shard_map/ppermute | solution.py:250
  4.5 3.9 %local_scores.1 = (bf16[32,128,128]{2,1,0:T(8,128)(2,1)S(1)}, f32[32,128,128]{2,1,0:T(8,128)S(1)}, f32[1,2,128,128]{3,2,1,0:T(8,128)S(1)}, bf16[128,512]{1,0:T(8,128)(2,1)S(1)}) custom-call(bf16[128,4096]{1,0:T(8,128)(2,1)} %q_hbm.1, bf16[128,512]{1,0:T(8,128)(2,1)} %k_hbm.1, bf16[128,512]{1,0:T(8,128)(2,1)} %v_hbm.1, f32[1,128]{1,0:T(1,128)} %bitcast.2, ...), custom_call_target="tpu_custom_call" | custom-call | tf_op jit(solution)/shard_map/local_scores/pallas_call | solution.py:254
  8.4 0.0 collective-permute-done.refs_0_
  8.4 1.3 %weights.1.weight_ref = bf16[32,128,256]{2,1,0:T(8,128)(2,1)S(1)} custom-call(bf16[32,128,128]{2,1,0:T(8,128)(2,1)S(1)} %get-tuple-element.9.rotated_ref, f32[32,128,128]{2,1,0:T(8,128)S(1)} %get-tuple-element.10.score_ref, f32[1,2,128,128]{3,2,1,0:T(8,128)S(1)} %get-tuple-element.11.table_ref, bf16[128,512]{1,0:T(8,128)(2,1)S(1)} %collective-permute-done.refs_0_), custom_call_target="tpu_custom_call" | custom-call | tf_op jit(solution)/shard_map/weights/pallas_call | solution.py:278
  9.6 0.1 collective-permute-done.1.refs_1_
  9.7 1.5 %mix_values.1 = bf16[128,4096]{1,0:T(8,128)(2,1)} custom-call(bf16[32,128,256]{2,1,0:T(8,128)(2,1)S(1)} %weights.1.weight_ref, bf16[128,512]{1,0:T(8,128)(2,1)S(1)} %get-tuple-element.12.refs_0_, bf16[128,512]{1,0:T(8,128)(2,1)S(1)} %collective-permute-done.1.refs_1_), custom_call_target="tpu_custom_call" | custom-call | tf_op jit(solution)/shard_map/mix_values/pallas_call | solution.py:286
Async XLA Ops:
  0.0 8.4 %collective-permute-start = (bf16[128,512]{1,0:T(8,128)(2,1)}, bf16[128,512]{1,0:T(8,128)(2,1)S(1)}, u32[]{:S(2)}, u32[]{:S(2)}) collective-permute-start(bf16[128,512]{1,0:T(8,128)(2,1)} %k_hbm.1), channel_id=1, source_target_pairs={{0,2},{2,4},{4,6},{6,8},{8,10},{10,12},{12,14},{14,15},{15,13},{13... | collective-permute-start | bytes 393224 | tf_op jit(solution)/shard_map/ppermute | solution.py:249
  2.9 6.8 %collective-permute-start.1 = (bf16[128,512]{1,0:T(8,128)(2,1)}, bf16[128,512]{1,0:T(8,128)(2,1)S(1)}, u32[]{:S(2)}, u32[]{:S(2)}) collective-permute-start(bf16[128,512]{1,0:T(8,128)(2,1)} %v_hbm.1), channel_id=1, source_target_pairs={{0,2},{2,4},{4,6},{6,8},{8,10},{10,12},{12,14},{14,15},{15,13},{13... | collective-permute-start | bytes 393224 | tf_op jit(solution)/shard_map/ppermute | solution.py:250

commit v4 on v3

--- a/solution.py
+++ b/solution.py
@@ -13,6 +13,7 @@
 ROPE_BASE = 1000000.0
 EPSILON = 1e-06
 DOT_HEADS = 4
+LAG = 1
 LOOP_A, LOOP_B, LOOP_C = False, False, False
 VMEM_LIMIT = 16 * 1024 * 1024
 
@@ -62,11 +63,18 @@
     return gain * (base_cos * cosine - base_sin * sine), turned_gain * (base_sin * cosine + base_cos * sine)
 
 
-def rotate_head(raw, cosine, sine):
+def half_turn(width):
+    rows = lax.broadcasted_iota(jnp.int32, (width, width), 0)
+    columns = lax.broadcasted_iota(jnp.int32, (width, width), 1)
+    swapped = jnp.where(columns < width // 2, columns + width // 2, columns - width // 2)
+    return (rows == swapped).astype(jnp.float32).astype(jnp.bfloat16)
+
+
+def rotate_head(raw, cosine, sine, swap):
     values = raw.astype(jnp.float32)
     width = values.shape[-1]
     square_sum = jnp.sum(values * values, axis=-1, keepdims=True)
-    turned = values * cosine + pltpu.roll(values, width // 2, 1) * sine
+    turned = values * cosine + matmul(raw, swap) * sine
     return (turned * lax.rsqrt(square_sum + width * EPSILON)).astype(jnp.bfloat16)
 
 
@@ -90,6 +98,15 @@
 
 def matmul_t(left, right):
     return lax.dot_general(left, right, (((1,), (1,)), ((), ())), preferred_element_type=jnp.float32)
+
+
+def start_store(stage_ref, out_hbm, out_sem, g):
+    place = columns_of(g, stage_ref.shape[2])
+    pltpu.make_async_copy(stage_ref.at[g], out_hbm.at[:, place], out_sem).start()
+
+
+def wait_stores(stage_ref, out_sem):
+    pltpu.make_async_copy(stage_ref, stage_ref, out_sem).wait()
 
 
 def local_kernel(
@@ -106,6 +123,7 @@
     score_ref,
     table_ref,
     value_ref,
+    out_hbm,
     q_ref,
     k_ref,
     q_gain_ref,
@@ -115,6 +133,8 @@
     small_sem,
     q_sem,
     v_sem,
+    stage_ref,
+    out_sem,
 ):
     heads, length, width = rotated_ref.shape
     kv_heads = k_ref.shape[1] // width
@@ -155,82 +175,115 @@
     rows = lax.broadcasted_iota(jnp.int32, (length, length), 0)
     columns = lax.broadcasted_iota(jnp.int32, (length, length), 1)
     own = columns <= rows
-    keys = [rotate_head(k_ref[:, columns_of(g, width)], k_cos, k_sin) for g in range(kv_heads)]
+    swap = half_turn(width)
+    keys = [rotate_head(k_ref[:, columns_of(g, width)], k_cos, k_sin, swap) for g in range(kv_heads)]
 
     def score(g):
         for i in range(group):
             scores = matmul_t(rotated_ref[g * group + i], keys[g])
-            score_ref[g * group + i] = jnp.where(own, scores, NEG_FILL)
-
-    for g in range(kv_heads):
-        q_copy(g).wait()
-        for i in range(group):
-            rotated_ref[g * group + i] = rotate_head(q_ref[g, :, i * width : (i + 1) * width], q_cos, q_sin)
-        if g > 0:
-            score(g - 1)
+            score_ref[g * group + i] = scores
+
+    first = 0
+    for count in [2, 2]:
+        some = range(first, first + count)
+        for g in some:
+            q_copy(g).wait()
+        for g in some:
+            for i in range(group):
+                rotated_ref[g * group + i] = rotate_head(q_ref[g, :, i * width : (i + 1) * width], q_cos, q_sin, swap)
+        for g in range(max(first - 1, 0), first + count - 1):
+            score(g)
+        first += count
     score(kv_heads - 1)
     v_copy.wait()
 
-
-def weight_kernel(cycle, span, rotated_ref, score_ref, table_ref, *refs):
+    @pl.when(stretch == 0)
+    def _():
+        to_exponent = math.log2(math.e) / math.sqrt(width)
+        ones = jnp.ones((length, width), jnp.bfloat16)
+        for g in range(kv_heads):
+            values = jnp.concatenate([value_ref[:, columns_of(g, width)], ones], axis=1)
+            for i in range(group):
+                tile = jnp.where(own, score_ref[g * group + i], NEG_FILL)
+                top = jnp.max(tile, axis=-1, keepdims=True)
+                mixed = matmul(jnp.exp2((tile - top) * to_exponent).astype(jnp.bfloat16), values)
+                mixed = mixed[:, :width] * (1.0 / mixed[:, width:])
+                stage_ref[g, :, columns_of(i, width)] = mixed.astype(jnp.bfloat16)
+            start_store(stage_ref, out_hbm, out_sem, g)
+        wait_stores(stage_ref, out_sem)
+
+
+def weight_kernel(cycle, span, *refs):
+    @pl.when(my_stretch(cycle) > 0)
+    def _():
+        later_weights(cycle, span, *refs)
+
+
+def later_weights(cycle, span, rotated_ref, score_ref, table_ref, *refs):
     key_refs = refs[:span]
     weight_ref = refs[span]
     heads, length, width = rotated_ref.shape
     kv_heads = key_refs[0].shape[1] // width
     group = heads // kv_heads
     stretch = my_stretch(cycle)
+    swap = half_turn(width)
     to_exponent = math.log2(math.e) / math.sqrt(width)
     rows = lax.broadcasted_iota(jnp.int32, (length, length), 0)
     columns = lax.broadcasted_iota(jnp.int32, (length, length), 1)
     own = columns <= rows
     near = columns <= jnp.where(stretch >= span, rows, length)
 
-    def one_group(g, carry):
-        keys = [
-            rotate_head(key_refs[d][:, columns_of(g, width)], table_ref[d, 0], table_ref[d, 1]) for d in range(span)
+    def scores_of(h, keys):
+        far = [matmul_t(rotated_ref[h], key) for key in keys]
+        tiles = [jnp.where(near, score_ref[h], far[span - 1])]
+        for d in range(span - 1):
+            tiles.append(jnp.where(stretch > d, far[d], NEG_FILL))
+        return tiles, jnp.max(functools.reduce(jnp.maximum, tiles), axis=-1, keepdims=True)
+
+    def weights_of(h, tiles, top):
+        weights = [jnp.exp2((tile - top) * to_exponent) for tile in tiles]
+        weights = [jnp.where(own, weights[0], 0.0), *weights[1:], jnp.where(own, 0.0, weights[0])]
+        weight_ref[h] = jnp.concatenate(weights, axis=1).astype(jnp.bfloat16)
+
+    keys = [
+        [
+            rotate_head(key_refs[d][:, columns_of(g, width)], table_ref[d, 0], table_ref[d, 1], swap)
+            for d in range(span)
         ]
-        for i in range(group):
-            h = g * group + i
-            far = [matmul_t(rotated_ref[h], keys[d]) for d in range(span)]
-            tiles = [jnp.where(near, score_ref[h], far[span - 1])]
-            for d in range(span - 1):
-                tiles.append(jnp.where(stretch > d, far[d], NEG_FILL))
-            top = jnp.max(functools.reduce(jnp.maximum, tiles), axis=-1, keepdims=True)
-            weights = [jnp.exp2((tile - top) * to_exponent) for tile in tiles]
-            weights = [jnp.where(own, weights[0], 0.0), *weights[1:], jnp.where(own, 0.0, weights[0])]
-            weight_ref[h] = jnp.concatenate(weights, axis=1).astype(jnp.bfloat16)
-        return carry
-
-    loop(LOOP_B, kv_heads, one_group)
-
-
-def mix_kernel(weight_ref, *refs):
+        for g in range(kv_heads)
+    ]
+    held = []
+    for h in range(heads):
+        held.append((h, *scores_of(h, keys[h // group])))
+        if len(held) > LAG:
+            weights_of(*held.pop(0))
+    for item in held:
+        weights_of(*item)
+
+
+def mix_kernel(cycle, weight_ref, *refs):
     out_hbm, stage_ref, out_sem = refs[-3:]
-    value_refs = refs[:-3]
+    value_refs = refs[:-4]
     heads, length, keys = weight_ref.shape
     kv_heads, _, group_width = stage_ref.shape
     group = heads // kv_heads
     width = group_width // group
-    ones = jnp.ones((keys, width), jnp.bfloat16)
-
-    def store(g):
-        return pltpu.make_async_copy(stage_ref.at[g], out_hbm.at[:, columns_of(g, group_width)], out_sem.at[g])
-
-    def one_group(g, carry):
-        values = jnp.concatenate([ref[:, columns_of(g, width)] for ref in value_refs], axis=0)
-        values = jnp.concatenate([values, ones], axis=1)
-        for first in range(0, group, DOT_HEADS):
-            weights = weight_ref[g * group + first : g * group + first + DOT_HEADS]
-            mixed = matmul(weights.reshape(DOT_HEADS * length, keys), values)
-            mixed = mixed[:, :width] * (1.0 / mixed[:, width:])
-            for i in range(DOT_HEADS):
-                stage_ref[g, :, columns_of(first + i, width)] = mixed[i * length : (i + 1) * length].astype(jnp.bfloat16)
-        store(g).start()
-        return carry
-
-    loop(LOOP_C, kv_heads, one_group)
-    for g in range(kv_heads):
-        store(g).wait()
+
+    @pl.when(my_stretch(cycle) > 0)
+    def _():
+        ones = jnp.ones((keys, width), jnp.bfloat16)
+        for g in range(kv_heads):
+            values = jnp.concatenate([ref[:, columns_of(g, width)] for ref in value_refs], axis=0)
+            values = jnp.concatenate([values, ones], axis=1)
+            for first in range(0, group, DOT_HEADS):
+                weights = weight_ref[g * group + first : g * group + first + DOT_HEADS]
+                mixed = matmul(weights.reshape(DOT_HEADS * length, keys), values)
+                mixed = mixed[:, :width] * (1.0 / mixed[:, width:])
+                for i in range(DOT_HEADS):
+                    part = mixed[i * length : (i + 1) * length].astype(jnp.bfloat16)
+                    stage_ref[g, :, columns_of(first + i, width)] = part
+            start_store(stage_ref, out_hbm, out_sem, g)
+        wait_stores(stage_ref, out_sem)
 
 
 def local(query_proj, key_proj, value_projection, query_gain, key_gain):
@@ -251,15 +304,16 @@
 
     base, offset = rotary_tables(2 * cycle, span, length, width)
     operands = (query_proj, key_proj, value_projection, query_gain[None], key_gain[None], base, offset)
-    rotated, scores, tables, values = pl.pallas_call(
+    rotated, scores, tables, values, out = pl.pallas_call(
         functools.partial(local_kernel, cycle, span),
         in_specs=[hbm] * 7,
-        out_specs=[vmem] * 4,
+        out_specs=[vmem] * 4 + [hbm],
         out_shape=[
             pltpu.VMEM((heads, length, width), jnp.bfloat16),
             pltpu.VMEM((heads, length, length), jnp.float32),
             pltpu.VMEM((span, 2, length, width), jnp.float32),
             pltpu.VMEM((length, kv_width), jnp.bfloat16),
+            jax.ShapeDtypeStruct(query_proj.shape, jnp.bfloat16),
         ],
         scratch_shapes=[
             pltpu.VMEM((kv_heads, length, query_width // kv_heads), jnp.bfloat16),
@@ -270,6 +324,8 @@
             pltpu.VMEM(offset.shape, jnp.float32),
             pltpu.SemaphoreType.DMA((5,)),
             pltpu.SemaphoreType.DMA((kv_heads,)),
+            pltpu.SemaphoreType.DMA,
+            pltpu.VMEM((kv_heads, length, query_width // kv_heads), jnp.bfloat16),
             pltpu.SemaphoreType.DMA,
         ],
         compiler_params=params,
@@ -284,17 +340,18 @@
         name="weights",
     )(rotated, scores, tables, *far_keys)
     return pl.pallas_call(
-        mix_kernel,
-        in_specs=[vmem] * (2 + span),
+        functools.partial(mix_kernel, cycle),
+        in_specs=[vmem] * (2 + span) + [hbm],
         out_specs=hbm,
         out_shape=jax.ShapeDtypeStruct(query_proj.shape, jnp.bfloat16),
+        input_output_aliases={2 + span: 0},
         scratch_shapes=[
             pltpu.VMEM((kv_heads, length, query_width // kv_heads), jnp.bfloat16),
-            pltpu.SemaphoreType.DMA((kv_heads,)),
+            pltpu.SemaphoreType.DMA,
         ],
         compiler_params=params,
         name="mix_values",
-    )(weights, values, *far_values)
+    )(weights, values, *far_values, out)
 
 
 def solution(mesh):

time: 11.3 us -> 10.7 us (0.947)
  the two profiles are of different devices: /device:TPU:0 before, /device:TPU:6 now
where the time goes in v4:
time: 10.7 us; the launch traced here: 10.6 us
  Pallas kernels  5.5 us (51%)
  starting transfers between devices  3.04 us (28%)
  waiting for transfers between devices  2.03 us (19%)
    pallas_call x1, Pallas kernels, local(): pl.pallas_call(functools.partial(local_kernel, cycle, span), in_specs=[hb...  2.95 us
    ppermute x1, waiting for transfers between devices, local(): lax.ppermute(key_proj, ('blk', 'uly'), route)  1.75 us
    ppermute x1, starting transfers between devices, local(): lax.ppermute(key_proj, ('blk', 'uly'), route)  1.55 us
    ppermute x1, starting transfers between devices, local(): lax.ppermute(value_projection, ('blk', 'uly'), route)  1.49 us
    pallas_call x1, Pallas kernels, local(): pl.pallas_call(functools.partial(mix_kernel, cycle), in_specs=[vmem] * (2...  1.43 us
    pallas_call x1, Pallas kernels, local(): pl.pallas_call(functools.partial(weight_kernel, cycle, span), in_specs=[v...  1.12 us
    ppermute x1, waiting for transfers between devices, local(): lax.ppermute(value_projection, ('blk', 'uly'), route)  0.28 us
  transfers between devices with their start and end apart: 2, of which 2 were waited for; matrix products, arithmetic and copies ran while one was open for 0% of the time, Pallas kernels for 38%

profile of v4, /device:TPU:6, one launch (start us, length us, event | category | flops | bytes accessed | tf_op | source)
XLA Modules:
  0.0 10.6 jit_solution(11573802451391009609)
XLA Ops:
  0.0 1.5 %collective-permute-start = (bf16[128,512]{1,0:T(8,128)(2,1)}, bf16[128,512]{1,0:T(8,128)(2,1)S(1)}, u32[]{:S(2)}, u32[]{:S(2)}) collective-permute-start(bf16[128,512]{1,0:T(8,128)(2,1)} %k_hbm.1), channel_id=1, source_target_pairs={{0,2},{2,4},{4,6},{6,8},{8,10},{10,12},{12,14},{14,15},{15,13},{13... | collective-permute-start | bytes 393224 | tf_op jit(solution)/shard_map/ppermute | solution.py:302
  1.5 1.5 %collective-permute-start.1 = (bf16[128,512]{1,0:T(8,128)(2,1)}, bf16[128,512]{1,0:T(8,128)(2,1)S(1)}, u32[]{:S(2)}, u32[]{:S(2)}) collective-permute-start(bf16[128,512]{1,0:T(8,128)(2,1)} %v_hbm.1), channel_id=1, source_target_pairs={{0,2},{2,4},{4,6},{6,8},{8,10},{10,12},{12,14},{14,15},{15,13},{13... | collective-permute-start | bytes 393224 | tf_op jit(solution)/shard_map/ppermute | solution.py:303
  3.0 3.0 %local_scores.1 = (bf16[32,128,128]{2,1,0:T(8,128)(2,1)S(1)}, f32[32,128,128]{2,1,0:T(8,128)S(1)}, f32[1,2,128,128]{3,2,1,0:T(8,128)S(1)}, bf16[128,512]{1,0:T(8,128)(2,1)S(1)}, bf16[128,4096]{1,0:T(8,128)(2,1)}) custom-call(bf16[128,4096]{1,0:T(8,128)(2,1)} %q_hbm.1, bf16[128,512]{1,0:T(8,128)(2,1)} %k_hbm.1, bf16[128,512]{1,0:T(8,128)(2,1)} %v_hbm.1, ...), custom_call_target="tpu_custom_call" | custom-call | tf_op jit(solution)/shard_map/local_scores/pallas_call | solution.py:307
  6.0 1.8 %collective-permute-done.refs_3_ = bf16[128,512]{1,0:T(8,128)(2,1)S(1)} collective-permute-done((bf16[128,512]{1,0:T(8,128)(2,1)}, bf16[128,512]{1,0:T(8,128)(2,1)S(1)}, u32[]{:S(2)}, u32[]{:S(2)}) %collective-permute-start) | collective-permute-done | bytes 131104 | tf_op jit(solution)/shard_map/ppermute | solution.py:302
  7.8 1.1 %weights.1.weight_ref = bf16[32,128,256]{2,1,0:T(8,128)(2,1)S(1)} custom-call(bf16[32,128,128]{2,1,0:T(8,128)(2,1)S(1)} %get-tuple-element.10.refs_0_, f32[32,128,128]{2,1,0:T(8,128)S(1)} %get-tuple-element.11.refs_1_, f32[1,2,128,128]{3,2,1,0:T(8,128)S(1)} %get-tuple-element.12.refs_2_, bf16[128,512]{1,0:T(8,128)(2,1)S(1)} %collective-permute-done.refs_3_), custom_call_target="tpu_custom_call" | custom-call | tf_op jit(solution)/shard_map/weights/pallas_call | solution.py:334
  8.9 0.3 %collective-permute-done.1.refs_1_ = bf16[128,512]{1,0:T(8,128)(2,1)S(1)} collective-permute-done((bf16[128,512]{1,0:T(8,128)(2,1)}, bf16[128,512]{1,0:T(8,128)(2,1)S(1)}, u32[]{:S(2)}, u32[]{:S(2)}) %collective-permute-start.1) | collective-permute-done | bytes 131104 | tf_op jit(solution)/shard_map/ppermute | solution.py:303
  9.2 1.4 %mix_values.1 = bf16[128,4096]{1,0:T(8,128)(2,1)} custom-call(bf16[32,128,256]{2,1,0:T(8,128)(2,1)S(1)} %weights.1.weight_ref, bf16[128,512]{1,0:T(8,128)(2,1)S(1)} %get-tuple-element.13.refs_0_, bf16[128,512]{1,0:T(8,128)(2,1)S(1)} %collective-permute-done.1.refs_1_, bf16[128,4096]{1,0:T(8,128)(2,1)} %get-tuple-element.14.refs_2_), custom_call_target="tpu_custom_call", output_to_operand_aliasing={{}: (3, {})} | custom-call | tf_op jit(solution)/shard_map/mix_values/pallas_call | solution.py:342
Async XLA Ops:
  0.0 7.8 %collective-permute-start = (bf16[128,512]{1,0:T(8,128)(2,1)}, bf16[128,512]{1,0:T(8,128)(2,1)S(1)}, u32[]{:S(2)}, u32[]{:S(2)}) collective-permute-start(bf16[128,512]{1,0:T(8,128)(2,1)} %k_hbm.1), channel_id=1, source_target_pairs={{0,2},{2,4},{4,6},{6,8},{8,10},{10,12},{12,14},{14,15},{15,13},{13... | collective-permute-start | bytes 393224 | tf_op jit(solution)/shard_map/ppermute | solution.py:302
  1.5 7.6 %collective-permute-start.1 = (bf16[128,512]{1,0:T(8,128)(2,1)}, bf16[128,512]{1,0:T(8,128)(2,1)S(1)}, u32[]{:S(2)}, u32[]{:S(2)}) collective-permute-start(bf16[128,512]{1,0:T(8,128)(2,1)} %v_hbm.1), channel_id=1, source_target_pairs={{0,2},{2,4},{4,6},{6,8},{8,10},{10,12},{12,14},{14,15},{15,13},{13... | collective-permute-start | bytes 393224 | tf_op jit(solution)/shard_map/ppermute | solution.py:303

commit v5 on v4

--- a/solution.py
+++ b/solution.py
@@ -12,8 +12,7 @@
 NEG_FILL = -1e30
 ROPE_BASE = 1000000.0
 EPSILON = 1e-06
-DOT_HEADS = 4
-LAG = 1
+PAIR = 2
 LOOP_A, LOOP_B, LOOP_C = False, False, False
 VMEM_LIMIT = 16 * 1024 * 1024
 
@@ -98,6 +97,20 @@
 
 def matmul_t(left, right):
     return lax.dot_general(left, right, (((1,), (1,)), ((), ())), preferred_element_type=jnp.float32)
+
+
+def pair_positions(length):
+    shape = (length, PAIR * length)
+    columns = lax.broadcasted_iota(jnp.int32, shape, 1)
+    return lax.broadcasted_iota(jnp.int32, shape, 0), lax.rem(columns, length)
+
+
+def put_pair(stage_ref, g, n, mixed):
+    width = mixed.shape[0]
+    turned = mixed.T
+    length = turned.shape[0] // PAIR
+    for i in range(PAIR):
+        stage_ref[g, :, columns_of(n * PAIR + i, width)] = turned[i * length : (i + 1) * length]
 
 
 def start_store(stage_ref, out_hbm, out_sem, g):
@@ -172,16 +185,13 @@
     k_cos, k_sin = gained_tables(bases[0], offset, k_gain)
     for d in range(span):
         table_ref[d, 0], table_ref[d, 1] = gained_tables(bases[d + 1], offset, k_gain)
-    rows = lax.broadcasted_iota(jnp.int32, (length, length), 0)
-    columns = lax.broadcasted_iota(jnp.int32, (length, length), 1)
-    own = columns <= rows
     swap = half_turn(width)
     keys = [rotate_head(k_ref[:, columns_of(g, width)], k_cos, k_sin, swap) for g in range(kv_heads)]
 
     def score(g):
-        for i in range(group):
-            scores = matmul_t(rotated_ref[g * group + i], keys[g])
-            score_ref[g * group + i] = scores
+        for n in range(g * group // PAIR, (g + 1) * group // PAIR):
+            queries = rotated_ref[n * PAIR : (n + 1) * PAIR].reshape(PAIR * length, width)
+            score_ref[n] = matmul_t(keys[g], queries)
 
     first = 0
     for count in [2, 2]:
@@ -199,16 +209,17 @@
 
     @pl.when(stretch == 0)
     def _():
+        keys_at, queries_at = pair_positions(length)
+        own = keys_at <= queries_at
         to_exponent = math.log2(math.e) / math.sqrt(width)
-        ones = jnp.ones((length, width), jnp.bfloat16)
         for g in range(kv_heads):
-            values = jnp.concatenate([value_ref[:, columns_of(g, width)], ones], axis=1)
-            for i in range(group):
-                tile = jnp.where(own, score_ref[g * group + i], NEG_FILL)
-                top = jnp.max(tile, axis=-1, keepdims=True)
-                mixed = matmul(jnp.exp2((tile - top) * to_exponent).astype(jnp.bfloat16), values)
-                mixed = mixed[:, :width] * (1.0 / mixed[:, width:])
-                stage_ref[g, :, columns_of(i, width)] = mixed.astype(jnp.bfloat16)
+            values = value_ref[:, columns_of(g, width)].T
+            for n in range(group // PAIR):
+                tile = jnp.where(own, score_ref[g * group // PAIR + n], NEG_FILL)
+                weights = jnp.exp2((tile - jnp.max(tile, axis=0, keepdims=True)) * to_exponent)
+                inverse = 1.0 / jnp.sum(weights, axis=0, keepdims=True)
+                mixed = matmul(values, weights.astype(jnp.bfloat16))
+                put_pair(stage_ref, g, n, (mixed * inverse).astype(jnp.bfloat16))
             start_store(stage_ref, out_hbm, out_sem, g)
         wait_stores(stage_ref, out_sem)
 
@@ -221,30 +232,15 @@
 
 def later_weights(cycle, span, rotated_ref, score_ref, table_ref, *refs):
     key_refs = refs[:span]
-    weight_ref = refs[span]
+    weight_ref, inverse_ref = refs[span:]
     heads, length, width = rotated_ref.shape
     kv_heads = key_refs[0].shape[1] // width
     group = heads // kv_heads
     stretch = my_stretch(cycle)
     swap = half_turn(width)
     to_exponent = math.log2(math.e) / math.sqrt(width)
-    rows = lax.broadcasted_iota(jnp.int32, (length, length), 0)
-    columns = lax.broadcasted_iota(jnp.int32, (length, length), 1)
-    own = columns <= rows
-    near = columns <= jnp.where(stretch >= span, rows, length)
-
-    def scores_of(h, keys):
-        far = [matmul_t(rotated_ref[h], key) for key in keys]
-        tiles = [jnp.where(near, score_ref[h], far[span - 1])]
-        for d in range(span - 1):
-            tiles.append(jnp.where(stretch > d, far[d], NEG_FILL))
-        return tiles, jnp.max(functools.reduce(jnp.maximum, tiles), axis=-1, keepdims=True)
-
-    def weights_of(h, tiles, top):
-        weights = [jnp.exp2((tile - top) * to_exponent) for tile in tiles]
-        weights = [jnp.where(own, weights[0], 0.0), *weights[1:], jnp.where(own, 0.0, weights[0])]
-        weight_ref[h] = jnp.concatenate(weights, axis=1).astype(jnp.bfloat16)
-
+    keys_at, queries_at = pair_positions(length)
+    own = keys_at <= queries_at
     keys = [
         [
             rotate_head(key_refs[d][:, columns_of(g, width)], table_ref[d, 0], table_ref[d, 1], swap)
@@ -252,36 +248,38 @@
         ]
         for g in range(kv_heads)
     ]
-    held = []
-    for h in range(heads):
-        held.append((h, *scores_of(h, keys[h // group])))
-        if len(held) > LAG:
-            weights_of(*held.pop(0))
-    for item in held:
-        weights_of(*item)
-
-
-def mix_kernel(cycle, weight_ref, *refs):
+    for n in range(heads // PAIR):
+        queries = rotated_ref[n * PAIR : (n + 1) * PAIR].reshape(PAIR * length, width)
+        far = [matmul_t(key, queries) for key in keys[n * PAIR // group]]
+        last = far[span - 1]
+        if span > 1:
+            last = jnp.where(stretch >= span, last, NEG_FILL)
+        tiles = [jnp.where(own, score_ref[n], last)]
+        for d in range(span - 1):
+            tiles.append(jnp.where(stretch > d, far[d], NEG_FILL))
+        top = jnp.max(functools.reduce(jnp.maximum, tiles), axis=0, keepdims=True)
+        weights = [jnp.exp2((tile - top) * to_exponent) for tile in tiles]
+        inverse_ref[n] = 1.0 / jnp.sum(functools.reduce(jnp.add, weights), axis=0, keepdims=True)
+        weights = [jnp.where(own, weights[0], 0.0), *weights[1:], jnp.where(own, 0.0, weights[0])]
+        for d in range(span + 1):
+            weight_ref[n, d * length : (d + 1) * length] = weights[d].astype(jnp.bfloat16)
+
+
+def mix_kernel(cycle, weight_ref, inverse_ref, *refs):
     out_hbm, stage_ref, out_sem = refs[-3:]
     value_refs = refs[:-4]
-    heads, length, keys = weight_ref.shape
-    kv_heads, _, group_width = stage_ref.shape
-    group = heads // kv_heads
-    width = group_width // group
+    pairs, keys, _ = weight_ref.shape
+    kv_heads, length, group_width = stage_ref.shape
+    group_pairs = pairs // kv_heads
+    width = group_width // group_pairs // PAIR
 
     @pl.when(my_stretch(cycle) > 0)
     def _():
-        ones = jnp.ones((keys, width), jnp.bfloat16)
         for g in range(kv_heads):
-            values = jnp.concatenate([ref[:, columns_of(g, width)] for ref in value_refs], axis=0)
-            values = jnp.concatenate([values, ones], axis=1)
-            for first in range(0, group, DOT_HEADS):
-                weights = weight_ref[g * group + first : g * group + first + DOT_HEADS]
-                mixed = matmul(weights.reshape(DOT_HEADS * length, keys), values)
-                mixed = mixed[:, :width] * (1.0 / mixed[:, width:])
-                for i in range(DOT_HEADS):
-                    part = mixed[i * length : (i + 1) * length].astype(jnp.bfloat16)
-                    stage_ref[g, :, columns_of(first + i, width)] = part
+            values = jnp.concatenate([ref[:, columns_of(g, width)].T for ref in value_refs], axis=1)
+            for n in range(group_pairs):
+                mixed = matmul(values, weight_ref[g * group_pairs + n]) * inverse_ref[g * group_pairs + n]
+                put_pair(stage_ref, g, n, mixed.astype(jnp.bfloat16))
             start_store(stage_ref, out_hbm, out_sem, g)
         wait_stores(stage_ref, out_sem)
 
@@ -310,7 +308,7 @@
         out_specs=[vmem] * 4 + [hbm],
         out_shape=[
             pltpu.VMEM((heads, length, width), jnp.bfloat16),
-            pltpu.VMEM((heads, length, length), jnp.float32),
+            pltpu.VMEM((heads // PAIR, length, PAIR * length), jnp.float32),
             pltpu.VMEM((span, 2, length, width), jnp.float32),
             pltpu.VMEM((length, kv_width), jnp.bfloat16),
             jax.ShapeDtypeStruct(query_proj.shape, jnp.bfloat16),
@@ -331,27 +329,30 @@
         compiler_params=params,
         name="local_scores",
     )(*[pltpu.with_memory_space_constraint(x, pltpu.HBM) for x in operands])
-    weights = pl.pallas_call(
+    weights, inverse = pl.pallas_call(
         functools.partial(weight_kernel, cycle, span),
         in_specs=[vmem] * (3 + span),
-        out_specs=vmem,
-        out_shape=pltpu.VMEM((heads, length, (span + 1) * length), jnp.bfloat16),
+        out_specs=[vmem] * 2,
+        out_shape=[
+            pltpu.VMEM((heads // PAIR, (span + 1) * length, PAIR * length), jnp.bfloat16),
+            pltpu.VMEM((heads // PAIR, 1, PAIR * length), jnp.float32),
+        ],
         compiler_params=params,
         name="weights",
     )(rotated, scores, tables, *far_keys)
     return pl.pallas_call(
         functools.partial(mix_kernel, cycle),
-        in_specs=[vmem] * (2 + span) + [hbm],
+        in_specs=[vmem] * (3 + span) + [hbm],
         out_specs=hbm,
         out_shape=jax.ShapeDtypeStruct(query_proj.shape, jnp.bfloat16),
-        input_output_aliases={2 + span: 0},
+        input_output_aliases={3 + span: 0},
         scratch_shapes=[
             pltpu.VMEM((kv_heads, length, query_width // kv_heads), jnp.bfloat16),
             pltpu.SemaphoreType.DMA,
         ],
         compiler_params=params,
         name="mix_values",
-    )(weights, values, *far_values, out)
+    )(weights, inverse, values, *far_values, out)
 
 
 def solution(mesh):

time: 10.7 us -> 10.6 us (level)
  Pallas kernels: 5.5 us -> 5.26 us
  waiting for transfers between devices: 2.03 us -> 2.15 us
    pallas_call x1, Pallas kernels: 2.95 us -> 2.71 us  [local(): pl.pallas_call(functools.partial(local_kernel, cycle, span), in_specs=[hb...]
    ppermute x1, waiting for transfers between devices: 1.75 us -> 2 us  [local(): lax.ppermute(key_proj, ('blk', 'uly'), route)]
    pallas_call x1, Pallas kernels: 1.12 us -> 1.24 us  [local(): pl.pallas_call(functools.partial(weight_kernel, cycle, span), in_specs=[v...]
    pallas_call x1, Pallas kernels: 1.43 us -> 1.31 us  [local(): pl.pallas_call(functools.partial(mix_kernel, cycle), in_specs=[vmem] * (3...]
    ppermute x1, waiting for transfers between devices: 0.28 us -> 0.16 us  [local(): lax.ppermute(value_projection, ('blk', 'uly'), route)]
where the time goes in v5:
time: 10.6 us; the launch traced here: 10.5 us
  Pallas kernels  5.26 us (50%)
  starting transfers between devices  3.04 us (29%)
  waiting for transfers between devices  2.15 us (20%)
    pallas_call x1, Pallas kernels, local(): pl.pallas_call(functools.partial(local_kernel, cycle, span), in_specs=[hb...  2.71 us
    ppermute x1, waiting for transfers between devices, local(): lax.ppermute(key_proj, ('blk', 'uly'), route)  2 us
    ppermute x1, starting transfers between devices, local(): lax.ppermute(key_proj, ('blk', 'uly'), route)  1.55 us
    ppermute x1, starting transfers between devices, local(): lax.ppermute(value_projection, ('blk', 'uly'), route)  1.49 us
    pallas_call x1, Pallas kernels, local(): pl.pallas_call(functools.partial(mix_kernel, cycle), in_specs=[vmem] * (3...  1.31 us
    pallas_call x1, Pallas kernels, local(): pl.pallas_call(functools.partial(weight_kernel, cycle, span), in_specs=[v...  1.24 us
  transfers between devices with their start and end apart: 2, of which 2 were waited for; matrix products, arithmetic and copies ran while one was open for 0% of the time, Pallas kernels for 38%

profile of v5, /device:TPU:6, one launch (start us, length us, event | category | flops | bytes accessed | tf_op | source)
XLA Modules:
  0.0 10.5 jit_solution(9196210293742152084)
XLA Ops:
  0.0 1.5 %collective-permute-start = (bf16[128,512]{1,0:T(8,128)(2,1)}, bf16[128,512]{1,0:T(8,128)(2,1)S(1)}, u32[]{:S(2)}, u32[]{:S(2)}) collective-permute-start(bf16[128,512]{1,0:T(8,128)(2,1)} %k_hbm.1), channel_id=1, source_target_pairs={{0,2},{2,4},{4,6},{6,8},{8,10},{10,12},{12,14},{14,15},{15,13},{13... | collective-permute-start | bytes 393224 | tf_op jit(solution)/shard_map/ppermute | solution.py:300
  1.5 1.5 %collective-permute-start.1 = (bf16[128,512]{1,0:T(8,128)(2,1)}, bf16[128,512]{1,0:T(8,128)(2,1)S(1)}, u32[]{:S(2)}, u32[]{:S(2)}) collective-permute-start(bf16[128,512]{1,0:T(8,128)(2,1)} %v_hbm.1), channel_id=1, source_target_pairs={{0,2},{2,4},{4,6},{6,8},{8,10},{10,12},{12,14},{14,15},{15,13},{13... | collective-permute-start | bytes 393224 | tf_op jit(solution)/shard_map/ppermute | solution.py:301
  3.0 2.7 %local_scores.1 = (bf16[32,128,128]{2,1,0:T(8,128)(2,1)S(1)}, f32[16,128,256]{2,1,0:T(8,128)S(1)}, f32[1,2,128,128]{3,2,1,0:T(8,128)S(1)}, bf16[128,512]{1,0:T(8,128)(2,1)S(1)}, bf16[128,4096]{1,0:T(8,128)(2,1)}) custom-call(bf16[128,4096]{1,0:T(8,128)(2,1)} %q_hbm.1, bf16[128,512]{1,0:T(8,128)(2,1)} %k_hbm.1, bf16[128,512]{1,0:T(8,128)(2,1)} %v_hbm.1, ...), custom_call_target="tpu_custom_call" | custom-call | tf_op jit(solution)/shard_map/local_scores/pallas_call | solution.py:305
  5.8 2.0 %collective-permute-done.refs_3_ = bf16[128,512]{1,0:T(8,128)(2,1)S(1)} collective-permute-done((bf16[128,512]{1,0:T(8,128)(2,1)}, bf16[128,512]{1,0:T(8,128)(2,1)S(1)}, u32[]{:S(2)}, u32[]{:S(2)}) %collective-permute-start) | collective-permute-done | bytes 131104 | tf_op jit(solution)/shard_map/ppermute | solution.py:300
  7.8 1.2 %weights.1 = (bf16[16,256,256]{2,1,0:T(8,128)(2,1)S(1)}, f32[16,1,256]{2,1,0:T(1,128)S(1)}) custom-call(bf16[32,128,128]{2,1,0:T(8,128)(2,1)S(1)} %get-tuple-element.12.refs_0_, f32[16,128,256]{2,1,0:T(8,128)S(1)} %get-tuple-element.13.refs_1_, f32[1,2,128,128]{3,2,1,0:T(8,128)S(1)} %get-tuple-element.14.refs_2_, ...), custom_call_target="tpu_custom_call" | custom-call | tf_op jit(solution)/shard_map/weights/pallas_call | solution.py:332
  9.0 0.2 %collective-permute-done.1.refs_1_ = bf16[128,512]{1,0:T(8,128)(2,1)S(1)} collective-permute-done((bf16[128,512]{1,0:T(8,128)(2,1)}, bf16[128,512]{1,0:T(8,128)(2,1)S(1)}, u32[]{:S(2)}, u32[]{:S(2)}) %collective-permute-start.1) | collective-permute-done | bytes 131104 | tf_op jit(solution)/shard_map/ppermute | solution.py:301
  9.2 1.3 %mix_values.1 = bf16[128,4096]{1,0:T(8,128)(2,1)} custom-call(bf16[16,256,256]{2,1,0:T(8,128)(2,1)S(1)} %get-tuple-element.15.weight_ref, f32[16,1,256]{2,1,0:T(1,128)S(1)} %get-tuple-element.16.inverse_ref, bf16[128,512]{1,0:T(8,128)(2,1)S(1)} %get-tuple-element.17.refs_0_, ...), custom_call_target="tpu_custom_call", output_to_operand_aliasing={{}: (4, {})} | custom-call | tf_op jit(solution)/shard_map/mix_values/pallas_call | solution.py:343
Async XLA Ops:
  0.0 7.8 %collective-permute-start = (bf16[128,512]{1,0:T(8,128)(2,1)}, bf16[128,512]{1,0:T(8,128)(2,1)S(1)}, u32[]{:S(2)}, u32[]{:S(2)}) collective-permute-start(bf16[128,512]{1,0:T(8,128)(2,1)} %k_hbm.1), channel_id=1, source_target_pairs={{0,2},{2,4},{4,6},{6,8},{8,10},{10,12},{12,14},{14,15},{15,13},{13... | collective-permute-start | bytes 393224 | tf_op jit(solution)/shard_map/ppermute | solution.py:300
  1.5 7.6 %collective-permute-start.1 = (bf16[128,512]{1,0:T(8,128)(2,1)}, bf16[128,512]{1,0:T(8,128)(2,1)S(1)}, u32[]{:S(2)}, u32[]{:S(2)}) collective-permute-start(bf16[128,512]{1,0:T(8,128)(2,1)} %v_hbm.1), channel_id=1, source_target_pairs={{0,2},{2,4},{4,6},{6,8},{8,10},{10,12},{12,14},{14,15},{15,13},{13... | collective-permute-start | bytes 393224 | tf_op jit(solution)/shard_map/ppermute | solution.py:301

commit v6 on v5

--- a/solution.py
+++ b/solution.py
@@ -13,6 +13,8 @@
 ROPE_BASE = 1000000.0
 EPSILON = 1e-06
 PAIR = 2
+DOT_PAIRS = 1
+LAG, MIX_LAG, MIX_PAIRS, KEY_AHEAD = 1, 2, 2, 16
 LOOP_A, LOOP_B, LOOP_C = False, False, False
 VMEM_LIMIT = 16 * 1024 * 1024
 
@@ -230,45 +232,78 @@
         later_weights(cycle, span, *refs)
 
 
-def later_weights(cycle, span, rotated_ref, score_ref, table_ref, *refs):
+def later_weights(cycle, span, rotated_ref, score_ref, table_ref, value_ref, *refs):
     key_refs = refs[:span]
-    weight_ref, inverse_ref = refs[span:]
+    weight_ref, mixed_ref, near_ref = refs[span:]
     heads, length, width = rotated_ref.shape
+    pairs = heads // PAIR
     kv_heads = key_refs[0].shape[1] // width
-    group = heads // kv_heads
+    group_pairs = pairs // kv_heads
     stretch = my_stretch(cycle)
     swap = half_turn(width)
     to_exponent = math.log2(math.e) / math.sqrt(width)
-    keys_at, queries_at = pair_positions(length)
-    own = keys_at <= queries_at
-    keys = [
-        [
-            rotate_head(key_refs[d][:, columns_of(g, width)], table_ref[d, 0], table_ref[d, 1], swap)
-            for d in range(span)
-        ]
-        for g in range(kv_heads)
-    ]
-    for n in range(heads // PAIR):
+    rows = lax.broadcasted_iota(jnp.int32, (length, length), 0)
+    columns = lax.broadcasted_iota(jnp.int32, (length, length), 1)
+    own = rows <= columns
+    near_part = (columns <= rows).astype(jnp.float32).astype(jnp.bfloat16)
+    near_part = jnp.concatenate([near_part] * PAIR, axis=0)
+    keys = []
+
+    def rotate_keys(g):
+        keys.append(
+            [
+                rotate_head(key_refs[d][:, columns_of(g, width)], table_ref[d, 0], table_ref[d, 1], swap)
+                for d in range(span)
+            ]
+        )
+
+    def weigh(n):
         queries = rotated_ref[n * PAIR : (n + 1) * PAIR].reshape(PAIR * length, width)
-        far = [matmul_t(key, queries) for key in keys[n * PAIR // group]]
-        last = far[span - 1]
+        tiles = [matmul_t(key, queries) for key in keys[n // group_pairs]]
         if span > 1:
-            last = jnp.where(stretch >= span, last, NEG_FILL)
-        tiles = [jnp.where(own, score_ref[n], last)]
-        for d in range(span - 1):
-            tiles.append(jnp.where(stretch > d, far[d], NEG_FILL))
+            tiles = [jnp.where(stretch > d, tiles[d], NEG_FILL) for d in range(span)]
+        merged = []
+        for i in range(PAIR):
+            place = columns_of(i, length)
+            merged.append(jnp.where(own, score_ref[n, :, place], tiles[span - 1][:, place]))
+        tiles[span - 1] = jnp.concatenate(merged, axis=1)
         top = jnp.max(functools.reduce(jnp.maximum, tiles), axis=0, keepdims=True)
         weights = [jnp.exp2((tile - top) * to_exponent) for tile in tiles]
-        inverse_ref[n] = 1.0 / jnp.sum(functools.reduce(jnp.add, weights), axis=0, keepdims=True)
-        weights = [jnp.where(own, weights[0], 0.0), *weights[1:], jnp.where(own, 0.0, weights[0])]
-        for d in range(span + 1):
-            weight_ref[n, d * length : (d + 1) * length] = weights[d].astype(jnp.bfloat16)
-
-
-def mix_kernel(cycle, weight_ref, inverse_ref, *refs):
+        inverse = 1.0 / jnp.sum(functools.reduce(jnp.add, weights), axis=0, keepdims=True)
+        return [(w * inverse).astype(jnp.bfloat16) for w in weights]
+
+    def put(n, weights):
+        for d in range(span):
+            turned = weights[d].T
+            if d == span - 1:
+                near = turned * near_part
+                near_ref[n] = near
+                turned = turned - near
+            weight_ref[n, :, d * length : (d + 1) * length] = turned
+
+    def mix_near(first):
+        some = slice(first, first + MIX_PAIRS)
+        near = near_ref[some].reshape(MIX_PAIRS * PAIR * length, length)
+        mixed = matmul(near, value_ref[:, columns_of(first // group_pairs, width)])
+        mixed_ref[some] = mixed.reshape(MIX_PAIRS, PAIR * length, width)
+
+    held = []
+    for n in range(pairs + max(LAG, MIX_LAG)):
+        while len(keys) < min(kv_heads, (n + KEY_AHEAD) // group_pairs + 1):
+            rotate_keys(len(keys))
+        if n < pairs:
+            held.append((n, weigh(n)))
+        if n >= LAG and held:
+            put(*held.pop(0))
+        mixed = n + 1 - MIX_LAG
+        if 0 < mixed <= pairs and mixed % MIX_PAIRS == 0:
+            mix_near(mixed - MIX_PAIRS)
+
+
+def mix_kernel(cycle, weight_ref, mixed_ref, *refs):
     out_hbm, stage_ref, out_sem = refs[-3:]
     value_refs = refs[:-4]
-    pairs, keys, _ = weight_ref.shape
+    pairs, rows, keys = weight_ref.shape
     kv_heads, length, group_width = stage_ref.shape
     group_pairs = pairs // kv_heads
     width = group_width // group_pairs // PAIR
@@ -276,10 +311,14 @@
     @pl.when(my_stretch(cycle) > 0)
     def _():
         for g in range(kv_heads):
-            values = jnp.concatenate([ref[:, columns_of(g, width)].T for ref in value_refs], axis=1)
-            for n in range(group_pairs):
-                mixed = matmul(values, weight_ref[g * group_pairs + n]) * inverse_ref[g * group_pairs + n]
-                put_pair(stage_ref, g, n, mixed.astype(jnp.bfloat16))
+            values = jnp.concatenate([ref[:, columns_of(g, width)] for ref in value_refs], axis=0)
+            for first in range(0, group_pairs, DOT_PAIRS):
+                some = slice(g * group_pairs + first, g * group_pairs + first + DOT_PAIRS)
+                mixed = matmul(weight_ref[some].reshape(DOT_PAIRS * rows, keys), values)
+                mixed = mixed + mixed_ref[some].reshape(DOT_PAIRS * rows, width)
+                for i in range(DOT_PAIRS * PAIR):
+                    part = mixed[i * length : (i + 1) * length].astype(jnp.bfloat16)
+                    stage_ref[g, :, columns_of(first * PAIR + i, width)] = part
             start_store(stage_ref, out_hbm, out_sem, g)
         wait_stores(stage_ref, out_sem)
 
@@ -298,7 +337,21 @@
 
     routes = [forward_route(d, cycle) for d in range(1, span + 1)]
     far_keys = [lax.ppermute(key_proj, ("blk", "uly"), route) for route in routes]
-    far_values = [lax.ppermute(value_projection, ("blk", "uly"), route) for route in routes]
+
+    def copy_kernel(source, target, sem):
+        copy = pltpu.make_async_copy(source, target, sem)
+        copy.start()
+        copy.wait()
+
+    v_copied = pl.pallas_call(
+        copy_kernel,
+        in_specs=[hbm],
+        out_specs=vmem,
+        out_shape=pltpu.VMEM(value_projection.shape, jnp.bfloat16),
+        scratch_shapes=[pltpu.SemaphoreType.DMA],
+        name="copy_values",
+    )(pltpu.with_memory_space_constraint(value_projection, pltpu.HBM))
+    far_values = [lax.ppermute(v_copied, ("blk", "uly"), route) for route in routes]
 
     base, offset = rotary_tables(2 * cycle, span, length, width)
     operands = (query_proj, key_proj, value_projection, query_gain[None], key_gain[None], base, offset)
@@ -329,30 +382,31 @@
         compiler_params=params,
         name="local_scores",
     )(*[pltpu.with_memory_space_constraint(x, pltpu.HBM) for x in operands])
-    weights, inverse = pl.pallas_call(
+    partial = pl.pallas_call(
         functools.partial(weight_kernel, cycle, span),
-        in_specs=[vmem] * (3 + span),
+        in_specs=[vmem] * (4 + span),
         out_specs=[vmem] * 2,
         out_shape=[
-            pltpu.VMEM((heads // PAIR, (span + 1) * length, PAIR * length), jnp.bfloat16),
-            pltpu.VMEM((heads // PAIR, 1, PAIR * length), jnp.float32),
+            pltpu.VMEM((heads // PAIR, PAIR * length, span * length), jnp.bfloat16),
+            pltpu.VMEM((heads // PAIR, PAIR * length, width), jnp.float32),
         ],
+        scratch_shapes=[pltpu.VMEM((heads // PAIR, PAIR * length, length), jnp.bfloat16)],
         compiler_params=params,
         name="weights",
-    )(rotated, scores, tables, *far_keys)
+    )(rotated, scores, tables, values, *far_keys)
     return pl.pallas_call(
         functools.partial(mix_kernel, cycle),
-        in_specs=[vmem] * (3 + span) + [hbm],
+        in_specs=[vmem] * (2 + span) + [hbm],
         out_specs=hbm,
         out_shape=jax.ShapeDtypeStruct(query_proj.shape, jnp.bfloat16),
-        input_output_aliases={3 + span: 0},
+        input_output_aliases={2 + span: 0},
         scratch_shapes=[
             pltpu.VMEM((kv_heads, length, query_width // kv_heads), jnp.bfloat16),
             pltpu.SemaphoreType.DMA,
         ],
         compiler_params=params,
         name="mix_values",
-    )(weights, inverse, values, *far_values, out)
+    )(*partial, *far_values, out)
 
 
 def solution(mesh):

time: 10.6 us -> 10.6 us (level)
  waiting for transfers between devices: 2.15 us -> 1.02 us
  Pallas kernels: 5.26 us -> 6.28 us
    ppermute x1, waiting for transfers between devices: 2 us -> 1.02 us  [local(): lax.ppermute(key_proj, ('blk', 'uly'), route)]
    pallas_call x1 -> x2, Pallas kernels: 1.31 us -> 2.11 us  [the longest x1 1.2 us: local(): pl.pallas_call(functools.partial(mix_kernel, cycle), in_specs=[vmem] * (2...]
    pallas_call x1, Pallas kernels: 1.24 us -> 1.46 us  [local(): pl.pallas_call(functools.partial(weight_kernel, cycle, span), in_specs=[v...]
    ppermute x1, waiting for transfers between devices: 0.16 us -> 0.01 us  [local(): lax.ppermute(v_copied, ('blk', 'uly'), route)]
  transfers between devices with their start and end apart: 2 -> 2, of which waited for: 2 -> 1; matrix products, arithmetic and copies ran while one was open for 0% -> 0% of each run, Pallas kernels for 38% -> 49%
where the time goes in v6:
time: 10.6 us; the launch traced here: 10.4 us
  Pallas kernels  6.28 us (59%)
  starting transfers between devices  3.1 us (29%)
  waiting for transfers between devices  1.02 us (10%)
    pallas_call x1, Pallas kernels, local(): pl.pallas_call(functools.partial(local_kernel, cycle, span), in_specs=[hb...  2.71 us
    ppermute x1, starting transfers between devices, local(): lax.ppermute(v_copied, ('blk', 'uly'), route)  1.55 us
    ppermute x1, starting transfers between devices, local(): lax.ppermute(key_proj, ('blk', 'uly'), route)  1.55 us
    pallas_call x1, Pallas kernels, local(): pl.pallas_call(functools.partial(weight_kernel, cycle, span), in_specs=[v...  1.46 us
    pallas_call x1, Pallas kernels, local(): pl.pallas_call(functools.partial(mix_kernel, cycle), in_specs=[vmem] * (2...  1.2 us
    ppermute x1, waiting for transfers between devices, local(): lax.ppermute(key_proj, ('blk', 'uly'), route)  1.02 us
    pallas_call x1, Pallas kernels, local(): pl.pallas_call(copy_kernel, in_specs=[hbm], out_specs=vmem, out_shape=plt...  0.91 us
  transfers between devices with their start and end apart: 2, of which 1 were waited for; matrix products, arithmetic and copies ran while one was open for 0% of the time, Pallas kernels for 49%

profile of v6, /device:TPU:6, one launch (start us, length us, event | category | flops | bytes accessed | tf_op | source)
XLA Modules:
  0.0 10.4 jit_solution(4395554941637436774)
XLA Ops:
  0.0 1.5 %collective-permute-start = (bf16[128,512]{1,0:T(8,128)(2,1)}, bf16[128,512]{1,0:T(8,128)(2,1)S(1)}, u32[]{:S(2)}, u32[]{:S(2)}) collective-permute-start(bf16[128,512]{1,0:T(8,128)(2,1)} %k_hbm.1), channel_id=1, source_target_pairs={{0,2},{2,4},{4,6},{6,8},{8,10},{10,12},{12,14},{14,15},{15,13},{13... | collective-permute-start | bytes 393224 | tf_op jit(solution)/shard_map/ppermute | solution.py:339
  1.5 0.9 %copy_values.1 = bf16[128,512]{1,0:T(8,128)(2,1)S(1)} custom-call(bf16[128,512]{1,0:T(8,128)(2,1)} %source.1), custom_call_target="tpu_custom_call" | custom-call | tf_op jit(solution)/shard_map/copy_values/pallas_call | solution.py:346
  2.5 1.5 %collective-permute-start.1 = (bf16[128,512]{1,0:T(8,128)(2,1)S(1)}, bf16[128,512]{1,0:T(8,128)(2,1)S(1)}, u32[]{:S(2)}, u32[]{:S(2)}) collective-permute-start(bf16[128,512]{1,0:T(8,128)(2,1)S(1)} %copy_values.1), channel_id=1, source_target_pairs={{0,2},{2,4},{4,6},{6,8},{8,10},{10,12},{12,14},{14,15},{15,13},{13... | collective-permute-start | bytes 393224 | tf_op jit(solution)/shard_map/ppermute | solution.py:354
  4.0 2.7 %local_scores.1 = (bf16[32,128,128]{2,1,0:T(8,128)(2,1)S(1)}, f32[16,128,256]{2,1,0:T(8,128)S(1)}, f32[1,2,128,128]{3,2,1,0:T(8,128)S(1)}, bf16[128,512]{1,0:T(8,128)(2,1)S(1)}, bf16[128,4096]{1,0:T(8,128)(2,1)}) custom-call(bf16[128,4096]{1,0:T(8,128)(2,1)} %q_hbm.1, bf16[128,512]{1,0:T(8,128)(2,1)} %k_hbm.1, bf16[128,512]{1,0:T(8,128)(2,1)} %source.1, ...), custom_call_target="tpu_custom_call" | custom-call | tf_op jit(solution)/shard_map/local_scores/pallas_call | solution.py:358
  6.7 1.0 %collective-permute-done.refs_4_ = bf16[128,512]{1,0:T(8,128)(2,1)S(1)} collective-permute-done((bf16[128,512]{1,0:T(8,128)(2,1)}, bf16[128,512]{1,0:T(8,128)(2,1)S(1)}, u32[]{:S(2)}, u32[]{:S(2)}) %collective-permute-start) | collective-permute-done | bytes 131104 | tf_op jit(solution)/shard_map/ppermute | solution.py:339
  7.8 1.5 %weights.1 = (bf16[16,256,128]{2,1,0:T(8,128)(2,1)S(1)}, f32[16,256,128]{2,1,0:T(8,128)S(1)}) custom-call(bf16[32,128,128]{2,1,0:T(8,128)(2,1)S(1)} %get-tuple-element.12.refs_0_, f32[16,128,256]{2,1,0:T(8,128)S(1)} %get-tuple-element.13.refs_1_, f32[1,2,128,128]{3,2,1,0:T(8,128)S(1)} %get-tuple-element.14.refs_2_, ...), custom_call_target="tpu_custom_call" | custom-call | tf_op jit(solution)/shard_map/weights/pallas_call | solution.py:385
  9.2 0.0 collective-permute-done.1.refs_0_
  9.2 1.2 %mix_values.1 = bf16[128,4096]{1,0:T(8,128)(2,1)} custom-call(bf16[16,256,128]{2,1,0:T(8,128)(2,1)S(1)} %get-tuple-element.16.weight_ref, f32[16,256,128]{2,1,0:T(8,128)S(1)} %get-tuple-element.17.mixed_ref, bf16[128,512]{1,0:T(8,128)(2,1)S(1)} %collective-permute-done.1.refs_0_, ...), custom_call_target="tpu_custom_call", output_to_operand_aliasing={{}: (3, {})} | custom-call | tf_op jit(solution)/shard_map/mix_values/pallas_call | solution.py:397
Async XLA Ops:
  0.0 7.8 %collective-permute-start = (bf16[128,512]{1,0:T(8,128)(2,1)}, bf16[128,512]{1,0:T(8,128)(2,1)S(1)}, u32[]{:S(2)}, u32[]{:S(2)}) collective-permute-start(bf16[128,512]{1,0:T(8,128)(2,1)} %k_hbm.1), channel_id=1, source_target_pairs={{0,2},{2,4},{4,6},{6,8},{8,10},{10,12},{12,14},{14,15},{15,13},{13... | collective-permute-start | bytes 393224 | tf_op jit(solution)/shard_map/ppermute | solution.py:339
  2.5 6.7 %collective-permute-start.1 = (bf16[128,512]{1,0:T(8,128)(2,1)S(1)}, bf16[128,512]{1,0:T(8,128)(2,1)S(1)}, u32[]{:S(2)}, u32[]{:S(2)}) collective-permute-start(bf16[128,512]{1,0:T(8,128)(2,1)S(1)} %copy_values.1), channel_id=1, source_target_pairs={{0,2},{2,4},{4,6},{6,8},{8,10},{10,12},{12,14},{14,15},{15,13},{13... | collective-permute-start | bytes 393224 | tf_op jit(solution)/shard_map/ppermute | solution.py:354

commit v7 on v5

--- a/solution.py
+++ b/solution.py
@@ -13,7 +13,8 @@
 ROPE_BASE = 1000000.0
 EPSILON = 1e-06
 PAIR = 2
-LOOP_A, LOOP_B, LOOP_C = False, False, False
+LAG = 1
+STORE_AFTER = (0, 2, 5, 8, 11, 13)
 VMEM_LIMIT = 16 * 1024 * 1024
 
 
@@ -81,14 +82,6 @@
     if isinstance(block, int):
         return slice(block * width, (block + 1) * width)
     return pl.ds(pl.multiple_of(block * width, width), width)
-
-
-def loop(rolled, count, body):
-    if rolled:
-        lax.fori_loop(0, count, body, None)
-    else:
-        for g in range(count):
-            body(g, None)
 
 
 def matmul(left, right):
@@ -139,6 +132,7 @@
     out_hbm,
     q_ref,
     k_ref,
+    v_ref,
     q_gain_ref,
     k_gain_ref,
     base_ref,
@@ -173,7 +167,7 @@
 
     for g in range(kv_heads):
         q_copy(g).start()
-    v_copy = pltpu.make_async_copy(v_hbm, value_ref, v_sem)
+    v_copy = pltpu.make_async_copy(v_hbm, v_ref, v_sem)
     v_copy.start()
     for copy in smalls:
         copy.wait()
@@ -206,6 +200,8 @@
         first += count
     score(kv_heads - 1)
     v_copy.wait()
+    for g in range(kv_heads):
+        value_ref[g] = v_ref[:, columns_of(g, width)].T
 
     @pl.when(stretch == 0)
     def _():
@@ -213,12 +209,11 @@
         own = keys_at <= queries_at
         to_exponent = math.log2(math.e) / math.sqrt(width)
         for g in range(kv_heads):
-            values = value_ref[:, columns_of(g, width)].T
             for n in range(group // PAIR):
                 tile = jnp.where(own, score_ref[g * group // PAIR + n], NEG_FILL)
                 weights = jnp.exp2((tile - jnp.max(tile, axis=0, keepdims=True)) * to_exponent)
                 inverse = 1.0 / jnp.sum(weights, axis=0, keepdims=True)
-                mixed = matmul(values, weights.astype(jnp.bfloat16))
+                mixed = matmul(value_ref[g], weights.astype(jnp.bfloat16))
                 put_pair(stage_ref, g, n, (mixed * inverse).astype(jnp.bfloat16))
             start_store(stage_ref, out_hbm, out_sem, g)
         wait_stores(stage_ref, out_sem)
@@ -239,8 +234,11 @@
     stretch = my_stretch(cycle)
     swap = half_turn(width)
     to_exponent = math.log2(math.e) / math.sqrt(width)
-    keys_at, queries_at = pair_positions(length)
-    own = keys_at <= queries_at
+    rows = lax.broadcasted_iota(jnp.int32, (length, length), 0)
+    columns = lax.broadcasted_iota(jnp.int32, (length, length), 1)
+    own = rows <= columns
+    near_part = own.astype(jnp.float32).astype(jnp.bfloat16)
+    near_part = jnp.concatenate([near_part] * PAIR, axis=1)
     keys = [
         [
             rotate_head(key_refs[d][:, columns_of(g, width)], table_ref[d, 0], table_ref[d, 1], swap)
@@ -251,36 +249,56 @@
     for n in range(heads // PAIR):
         queries = rotated_ref[n * PAIR : (n + 1) * PAIR].reshape(PAIR * length, width)
         far = [matmul_t(key, queries) for key in keys[n * PAIR // group]]
-        last = far[span - 1]
         if span > 1:
-            last = jnp.where(stretch >= span, last, NEG_FILL)
-        tiles = [jnp.where(own, score_ref[n], last)]
-        for d in range(span - 1):
-            tiles.append(jnp.where(stretch > d, far[d], NEG_FILL))
+            far = [jnp.where(stretch > d, far[d], NEG_FILL) for d in range(span)]
+        merged = []
+        for i in range(PAIR):
+            place = columns_of(i, length)
+            merged.append(jnp.where(own, score_ref[n, :, place], far[span - 1][:, place]))
+        tiles = [*far[: span - 1], jnp.concatenate(merged, axis=1)]
         top = jnp.max(functools.reduce(jnp.maximum, tiles), axis=0, keepdims=True)
         weights = [jnp.exp2((tile - top) * to_exponent) for tile in tiles]
-        inverse_ref[n] = 1.0 / jnp.sum(functools.reduce(jnp.add, weights), axis=0, keepdims=True)
-        weights = [jnp.where(own, weights[0], 0.0), *weights[1:], jnp.where(own, 0.0, weights[0])]
-        for d in range(span + 1):
-            weight_ref[n, d * length : (d + 1) * length] = weights[d].astype(jnp.bfloat16)
-
-
-def mix_kernel(cycle, weight_ref, inverse_ref, *refs):
+        inverse = 1.0 / jnp.sum(functools.reduce(jnp.add, weights), axis=0, keepdims=True)
+        inverse_ref[n] = inverse
+        weights = [w.astype(jnp.bfloat16) for w in weights]
+        near = weights[span - 1] * near_part
+        weights[span - 1] = weights[span - 1] - near
+        for d, part in enumerate([near, *weights]):
+            weight_ref[n, d * length : (d + 1) * length] = part
+
+
+def mix_kernel(cycle, weight_ref, inverse_ref, own_value_ref, *refs):
     out_hbm, stage_ref, out_sem = refs[-3:]
     value_refs = refs[:-4]
-    pairs, keys, _ = weight_ref.shape
-    kv_heads, length, group_width = stage_ref.shape
+    pairs = weight_ref.shape[0]
+    kv_heads, width, _ = own_value_ref.shape
     group_pairs = pairs // kv_heads
-    width = group_width // group_pairs // PAIR
 
     @pl.when(my_stretch(cycle) > 0)
     def _():
-        for g in range(kv_heads):
-            values = jnp.concatenate([ref[:, columns_of(g, width)].T for ref in value_refs], axis=1)
-            for n in range(group_pairs):
-                mixed = matmul(values, weight_ref[g * group_pairs + n]) * inverse_ref[g * group_pairs + n]
-                put_pair(stage_ref, g, n, mixed.astype(jnp.bfloat16))
-            start_store(stage_ref, out_hbm, out_sem, g)
+        values, held, ready = [], [], []
+
+        def mixed_pair(n):
+            g = n // group_pairs
+            if g == len(values):
+                parts = [ref[:, columns_of(g, width)].T for ref in value_refs]
+                values.append(jnp.concatenate([own_value_ref[g], *parts], axis=1))
+            return (matmul(values[g], weight_ref[n]) * inverse_ref[n]).astype(jnp.bfloat16)
+
+        def store_pair(n, mixed):
+            put_pair(stage_ref, n, 0, mixed)
+            ready.append(n)
+            if n in STORE_AFTER or n == pairs - 1:
+                for m in ready:
+                    start_store(stage_ref, out_hbm, out_sem, m)
+                ready.clear()
+
+        for n in range(pairs):
+            held.append((n, mixed_pair(n)))
+            if len(held) > LAG:
+                store_pair(*held.pop(0))
+        for item in held:
+            store_pair(*item)
         wait_stores(stage_ref, out_sem)
 
 
@@ -310,11 +328,12 @@
             pltpu.VMEM((heads, length, width), jnp.bfloat16),
             pltpu.VMEM((heads // PAIR, length, PAIR * length), jnp.float32),
             pltpu.VMEM((span, 2, length, width), jnp.float32),
-            pltpu.VMEM((length, kv_width), jnp.bfloat16),
+            pltpu.VMEM((kv_heads, width, length), jnp.bfloat16),
             jax.ShapeDtypeStruct(query_proj.shape, jnp.bfloat16),
         ],
         scratch_shapes=[
             pltpu.VMEM((kv_heads, length, query_width // kv_heads), jnp.bfloat16),
+            pltpu.VMEM((length, kv_width), jnp.bfloat16),
             pltpu.VMEM((length, kv_width), jnp.bfloat16),
             pltpu.VMEM((1, width), jnp.float32),
             pltpu.VMEM((1, width), jnp.float32),
@@ -347,7 +366,7 @@
         out_shape=jax.ShapeDtypeStruct(query_proj.shape, jnp.bfloat16),
         input_output_aliases={3 + span: 0},
         scratch_shapes=[
-            pltpu.VMEM((kv_heads, length, query_width // kv_heads), jnp.bfloat16),
+            pltpu.VMEM((heads // PAIR, length, PAIR * width), jnp.bfloat16),
             pltpu.SemaphoreType.DMA,
         ],
         compiler_params=params,

time: 10.6 us -> 10.6 us (level)
  Pallas kernels: 5.26 us -> 5.14 us
    ppermute x1, waiting for transfers between devices: 0.16 us -> 0.33 us  [local(): lax.ppermute(value_projection, ('blk', 'uly'), route)]
    pallas_call x1, Pallas kernels: 1.24 us -> 1.07 us  [local(): pl.pallas_call(functools.partial(weight_kernel, cycle, span), in_specs=[v...]
  transfers between devices with their start and end apart: 2 -> 2, of which waited for: 2 -> 2; matrix products, arithmetic and copies ran while one was open for 0% -> 0% of each run, Pallas kernels for 38% -> 37%
where the time goes in v7:
time: 10.6 us; the launch traced here: 10.4 us
  Pallas kernels  5.14 us (48%)
  starting transfers between devices  3.04 us (29%)
  waiting for transfers between devices  2.24 us (21%)
    pallas_call x1, Pallas kernels, local(): pl.pallas_call(functools.partial(local_kernel, cycle, span), in_specs=[hb...  2.79 us
    ppermute x1, waiting for transfers between devices, local(): lax.ppermute(key_proj, ('blk', 'uly'), route)  1.91 us
    ppermute x1, starting transfers between devices, local(): lax.ppermute(key_proj, ('blk', 'uly'), route)  1.55 us
    ppermute x1, starting transfers between devices, local(): lax.ppermute(value_projection, ('blk', 'uly'), route)  1.49 us
    pallas_call x1, Pallas kernels, local(): pl.pallas_call(functools.partial(mix_kernel, cycle), in_specs=[vmem] * (3...  1.28 us
    pallas_call x1, Pallas kernels, local(): pl.pallas_call(functools.partial(weight_kernel, cycle, span), in_specs=[v...  1.07 us
    ppermute x1, waiting for transfers between devices, local(): lax.ppermute(value_projection, ('blk', 'uly'), route)  0.33 us
  transfers between devices with their start and end apart: 2, of which 2 were waited for; matrix products, arithmetic and copies ran while one was open for 0% of the time, Pallas kernels for 37%

profile of v7, /device:TPU:6, one launch (start us, length us, event | category | flops | bytes accessed | tf_op | source)
XLA Modules:
  0.0 10.4 jit_solution(12897737970111912666)
XLA Ops:
  0.0 1.5 %collective-permute-start = (bf16[128,512]{1,0:T(8,128)(2,1)}, bf16[128,512]{1,0:T(8,128)(2,1)S(1)}, u32[]{:S(2)}, u32[]{:S(2)}) collective-permute-start(bf16[128,512]{1,0:T(8,128)(2,1)} %k_hbm.1), channel_id=1, source_target_pairs={{0,2},{2,4},{4,6},{6,8},{8,10},{10,12},{12,14},{14,15},{15,13},{13... | collective-permute-start | bytes 393224 | tf_op jit(solution)/shard_map/ppermute | solution.py:318
  1.5 1.5 %collective-permute-start.1 = (bf16[128,512]{1,0:T(8,128)(2,1)}, bf16[128,512]{1,0:T(8,128)(2,1)S(1)}, u32[]{:S(2)}, u32[]{:S(2)}) collective-permute-start(bf16[128,512]{1,0:T(8,128)(2,1)} %v_hbm.1), channel_id=1, source_target_pairs={{0,2},{2,4},{4,6},{6,8},{8,10},{10,12},{12,14},{14,15},{15,13},{13... | collective-permute-start | bytes 393224 | tf_op jit(solution)/shard_map/ppermute | solution.py:319
  3.0 2.8 %local_scores.1 = (bf16[32,128,128]{2,1,0:T(8,128)(2,1)S(1)}, f32[16,128,256]{2,1,0:T(8,128)S(1)}, f32[1,2,128,128]{3,2,1,0:T(8,128)S(1)}, bf16[4,128,128]{2,1,0:T(8,128)(2,1)S(1)}, bf16[128,4096]{1,0:T(8,128)(2,1)}) custom-call(bf16[128,4096]{1,0:T(8,128)(2,1)} %q_hbm.1, bf16[128,512]{1,0:T(8,128)(2,1)} %k_hbm.1, bf16[128,512]{1,0:T(8,128)(2,1)} %v_hbm.1, ...), custom_call_target="tpu_custom_call" | custom-call | tf_op jit(solution)/shard_map/local_scores/pallas_call | solution.py:323
  5.8 1.9 %collective-permute-done.refs_3_ = bf16[128,512]{1,0:T(8,128)(2,1)S(1)} collective-permute-done((bf16[128,512]{1,0:T(8,128)(2,1)}, bf16[128,512]{1,0:T(8,128)(2,1)S(1)}, u32[]{:S(2)}, u32[]{:S(2)}) %collective-permute-start) | collective-permute-done | bytes 131104 | tf_op jit(solution)/shard_map/ppermute | solution.py:318
  7.8 1.1 %weights.1 = (bf16[16,256,256]{2,1,0:T(8,128)(2,1)S(1)}, f32[16,1,256]{2,1,0:T(1,128)S(1)}) custom-call(bf16[32,128,128]{2,1,0:T(8,128)(2,1)S(1)} %get-tuple-element.12.refs_0_, f32[16,128,256]{2,1,0:T(8,128)S(1)} %get-tuple-element.13.refs_1_, f32[1,2,128,128]{3,2,1,0:T(8,128)S(1)} %get-tuple-element.14.refs_2_, ...), custom_call_target="tpu_custom_call" | custom-call | tf_op jit(solution)/shard_map/weights/pallas_call | solution.py:351
  8.8 0.3 %collective-permute-done.1.refs_0_ = bf16[128,512]{1,0:T(8,128)(2,1)S(1)} collective-permute-done((bf16[128,512]{1,0:T(8,128)(2,1)}, bf16[128,512]{1,0:T(8,128)(2,1)S(1)}, u32[]{:S(2)}, u32[]{:S(2)}) %collective-permute-start.1) | collective-permute-done | bytes 131104 | tf_op jit(solution)/shard_map/ppermute | solution.py:319
  9.2 1.3 %mix_values.1 = bf16[128,4096]{1,0:T(8,128)(2,1)} custom-call(bf16[16,256,256]{2,1,0:T(8,128)(2,1)S(1)} %get-tuple-element.15.weight_ref, f32[16,1,256]{2,1,0:T(1,128)S(1)} %get-tuple-element.16.inverse_ref, bf16[4,128,128]{2,1,0:T(8,128)(2,1)S(1)} %get-tuple-element.17.own_value_ref, ...), custom_call_target="tpu_custom_call", output_to_operand_aliasing={{}: (4, {})} | custom-call | tf_op jit(solution)/shard_map/mix_values/pallas_call | solution.py:362
Async XLA Ops:
  0.0 7.8 %collective-permute-start = (bf16[128,512]{1,0:T(8,128)(2,1)}, bf16[128,512]{1,0:T(8,128)(2,1)S(1)}, u32[]{:S(2)}, u32[]{:S(2)}) collective-permute-start(bf16[128,512]{1,0:T(8,128)(2,1)} %k_hbm.1), channel_id=1, source_target_pairs={{0,2},{2,4},{4,6},{6,8},{8,10},{10,12},{12,14},{14,15},{15,13},{13... | collective-permute-start | bytes 393224 | tf_op jit(solution)/shard_map/ppermute | solution.py:318
  1.5 7.6 %collective-permute-start.1 = (bf16[128,512]{1,0:T(8,128)(2,1)}, bf16[128,512]{1,0:T(8,128)(2,1)S(1)}, u32[]{:S(2)}, u32[]{:S(2)}) collective-permute-start(bf16[128,512]{1,0:T(8,128)(2,1)} %v_hbm.1), channel_id=1, source_target_pairs={{0,2},{2,4},{4,6},{6,8},{8,10},{10,12},{12,14},{14,15},{15,13},{13... | collective-permute-start | bytes 393224 | tf_op jit(solution)/shard_map/ppermute | solution.py:319

commit v8 on v7

--- a/solution.py
+++ b/solution.py
@@ -225,9 +225,9 @@
         later_weights(cycle, span, *refs)
 
 
-def later_weights(cycle, span, rotated_ref, score_ref, table_ref, *refs):
+def later_weights(cycle, span, rotated_ref, score_ref, table_ref, own_value_ref, *refs):
     key_refs = refs[:span]
-    weight_ref, inverse_ref = refs[span:]
+    weight_ref, mixed_ref, inverse_ref = refs[span:]
     heads, length, width = rotated_ref.shape
     kv_heads = key_refs[0].shape[1] // width
     group = heads // kv_heads
@@ -263,15 +263,17 @@
         weights = [w.astype(jnp.bfloat16) for w in weights]
         near = weights[span - 1] * near_part
         weights[span - 1] = weights[span - 1] - near
-        for d, part in enumerate([near, *weights]):
-            weight_ref[n, d * length : (d + 1) * length] = part
-
-
-def mix_kernel(cycle, weight_ref, inverse_ref, own_value_ref, *refs):
+        mixed_ref[n] = matmul(own_value_ref[n * PAIR // group], near) * inverse
+        for d in range(span):
+            weight_ref[n, d * length : (d + 1) * length] = weights[d]
+
+
+def mix_kernel(cycle, weight_ref, mixed_ref, inverse_ref, *refs):
     out_hbm, stage_ref, out_sem = refs[-3:]
     value_refs = refs[:-4]
     pairs = weight_ref.shape[0]
-    kv_heads, width, _ = own_value_ref.shape
+    width = mixed_ref.shape[1]
+    kv_heads = value_refs[0].shape[1] // width
     group_pairs = pairs // kv_heads
 
     @pl.when(my_stretch(cycle) > 0)
@@ -282,8 +284,8 @@
             g = n // group_pairs
             if g == len(values):
                 parts = [ref[:, columns_of(g, width)].T for ref in value_refs]
-                values.append(jnp.concatenate([own_value_ref[g], *parts], axis=1))
-            return (matmul(values[g], weight_ref[n]) * inverse_ref[n]).astype(jnp.bfloat16)
+                values.append(jnp.concatenate(parts, axis=1))
+            return (matmul(values[g], weight_ref[n]) * inverse_ref[n] + mixed_ref[n]).astype(jnp.bfloat16)
 
         def store_pair(n, mixed):
             put_pair(stage_ref, n, 0, mixed)
@@ -348,17 +350,18 @@
         compiler_params=params,
         name="local_scores",
     )(*[pltpu.with_memory_space_constraint(x, pltpu.HBM) for x in operands])
-    weights, inverse = pl.pallas_call(
+    partial = pl.pallas_call(
         functools.partial(weight_kernel, cycle, span),
-        in_specs=[vmem] * (3 + span),
-        out_specs=[vmem] * 2,
+        in_specs=[vmem] * (4 + span),
+        out_specs=[vmem] * 3,
         out_shape=[
-            pltpu.VMEM((heads // PAIR, (span + 1) * length, PAIR * length), jnp.bfloat16),
+            pltpu.VMEM((heads // PAIR, span * length, PAIR * length), jnp.bfloat16),
+            pltpu.VMEM((heads // PAIR, width, PAIR * length), jnp.float32),
             pltpu.VMEM((heads // PAIR, 1, PAIR * length), jnp.float32),
         ],
         compiler_params=params,
         name="weights",
-    )(rotated, scores, tables, *far_keys)
+    )(rotated, scores, tables, values, *far_keys)
     return pl.pallas_call(
         functools.partial(mix_kernel, cycle),
         in_specs=[vmem] * (3 + span) + [hbm],
@@ -371,7 +374,7 @@
         ],
         compiler_params=params,
         name="mix_values",
-    )(weights, inverse, values, *far_values, out)
+    )(*partial, *far_values, out)
 
 
 def solution(mesh):

time: 10.6 us -> 10.6 us (level)
  waiting for transfers between devices: 2.24 us -> 1.97 us
  Pallas kernels: 5.14 us -> 5.4 us
    ppermute x1, waiting for transfers between devices: 0.33 us -> 0.06 us  [local(): lax.ppermute(value_projection, ('blk', 'uly'), route)]
    pallas_call x1, Pallas kernels: 1.07 us -> 1.34 us  [local(): pl.pallas_call(functools.partial(weight_kernel, cycle, span), in_specs=[v...]
  transfers between devices with their start and end apart: 2 -> 2, of which waited for: 2 -> 2; matrix products, arithmetic and copies ran while one was open for 0% -> 0% of each run, Pallas kernels for 37% -> 40%
where the time goes in v8:
time: 10.6 us; the launch traced here: 10.4 us
  Pallas kernels  5.4 us (51%)
  starting transfers between devices  3.04 us (29%)
  waiting for transfers between devices  1.97 us (19%)
    pallas_call x1, Pallas kernels, local(): pl.pallas_call(functools.partial(local_kernel, cycle, span), in_specs=[hb...  2.79 us
    ppermute x1, waiting for transfers between devices, local(): lax.ppermute(key_proj, ('blk', 'uly'), route)  1.91 us
    ppermute x1, starting transfers between devices, local(): lax.ppermute(key_proj, ('blk', 'uly'), route)  1.55 us
    ppermute x1, starting transfers between devices, local(): lax.ppermute(value_projection, ('blk', 'uly'), route)  1.49 us
    pallas_call x1, Pallas kernels, local(): pl.pallas_call(functools.partial(weight_kernel, cycle, span), in_specs=[v...  1.34 us
    pallas_call x1, Pallas kernels, local(): pl.pallas_call(functools.partial(mix_kernel, cycle), in_specs=[vmem] * (3...  1.27 us
  transfers between devices with their start and end apart: 2, of which 2 were waited for; matrix products, arithmetic and copies ran while one was open for 0% of the time, Pallas kernels for 40%

profile of v8, /device:TPU:6, one launch (start us, length us, event | category | flops | bytes accessed | tf_op | source)
XLA Modules:
  0.0 10.4 jit_solution(1621050342826395158)
XLA Ops:
  0.0 1.5 %collective-permute-start = (bf16[128,512]{1,0:T(8,128)(2,1)}, bf16[128,512]{1,0:T(8,128)(2,1)S(1)}, u32[]{:S(2)}, u32[]{:S(2)}) collective-permute-start(bf16[128,512]{1,0:T(8,128)(2,1)} %k_hbm.1), channel_id=1, source_target_pairs={{0,2},{2,4},{4,6},{6,8},{8,10},{10,12},{12,14},{14,15},{15,13},{13... | collective-permute-start | bytes 393224 | tf_op jit(solution)/shard_map/ppermute | solution.py:320
  1.5 1.5 %collective-permute-start.1 = (bf16[128,512]{1,0:T(8,128)(2,1)}, bf16[128,512]{1,0:T(8,128)(2,1)S(1)}, u32[]{:S(2)}, u32[]{:S(2)}) collective-permute-start(bf16[128,512]{1,0:T(8,128)(2,1)} %v_hbm.1), channel_id=1, source_target_pairs={{0,2},{2,4},{4,6},{6,8},{8,10},{10,12},{12,14},{14,15},{15,13},{13... | collective-permute-start | bytes 393224 | tf_op jit(solution)/shard_map/ppermute | solution.py:321
  3.0 2.8 %local_scores.1 = (bf16[32,128,128]{2,1,0:T(8,128)(2,1)S(1)}, f32[16,128,256]{2,1,0:T(8,128)S(1)}, f32[1,2,128,128]{3,2,1,0:T(8,128)S(1)}, bf16[4,128,128]{2,1,0:T(8,128)(2,1)S(1)}, bf16[128,4096]{1,0:T(8,128)(2,1)}) custom-call(bf16[128,4096]{1,0:T(8,128)(2,1)} %q_hbm.1, bf16[128,512]{1,0:T(8,128)(2,1)} %k_hbm.1, bf16[128,512]{1,0:T(8,128)(2,1)} %v_hbm.1, ...), custom_call_target="tpu_custom_call" | custom-call | tf_op jit(solution)/shard_map/local_scores/pallas_call | solution.py:325
  5.8 1.9 %collective-permute-done.refs_4_ = bf16[128,512]{1,0:T(8,128)(2,1)S(1)} collective-permute-done((bf16[128,512]{1,0:T(8,128)(2,1)}, bf16[128,512]{1,0:T(8,128)(2,1)S(1)}, u32[]{:S(2)}, u32[]{:S(2)}) %collective-permute-start) | collective-permute-done | bytes 131104 | tf_op jit(solution)/shard_map/ppermute | solution.py:320
  7.8 1.3 %weights.1 = (bf16[16,128,256]{2,1,0:T(8,128)(2,1)S(1)}, f32[16,128,256]{2,1,0:T(8,128)S(1)}, f32[16,1,256]{2,1,0:T(1,128)S(1)}) custom-call(bf16[32,128,128]{2,1,0:T(8,128)(2,1)S(1)} %get-tuple-element.13.refs_0_, f32[16,128,256]{2,1,0:T(8,128)S(1)} %get-tuple-element.14.refs_1_, f32[1,2,128,128]{3,2,1,0:T(8,128)S(1)} %get-tuple-element.15.refs_2_, ...), custom_call_target="tpu_custom_call" | custom-call | tf_op jit(solution)/shard_map/weights/pallas_call | solution.py:353
  9.1 0.1 collective-permute-done.1.refs_0_
  9.2 1.3 %mix_values.1 = bf16[128,4096]{1,0:T(8,128)(2,1)} custom-call(bf16[16,128,256]{2,1,0:T(8,128)(2,1)S(1)} %get-tuple-element.17.weight_ref, f32[16,128,256]{2,1,0:T(8,128)S(1)} %get-tuple-element.18.mixed_ref, f32[16,1,256]{2,1,0:T(1,128)S(1)} %get-tuple-element.19.inverse_ref, ...), custom_call_target="tpu_custom_call", output_to_operand_aliasing={{}: (4, {})} | custom-call | tf_op jit(solution)/shard_map/mix_values/pallas_call | solution.py:365
Async XLA Ops:
  0.0 7.8 %collective-permute-start = (bf16[128,512]{1,0:T(8,128)(2,1)}, bf16[128,512]{1,0:T(8,128)(2,1)S(1)}, u32[]{:S(2)}, u32[]{:S(2)}) collective-permute-start(bf16[128,512]{1,0:T(8,128)(2,1)} %k_hbm.1), channel_id=1, source_target_pairs={{0,2},{2,4},{4,6},{6,8},{8,10},{10,12},{12,14},{14,15},{15,13},{13... | collective-permute-start | bytes 393224 | tf_op jit(solution)/shard_map/ppermute | solution.py:320
  1.5 7.6 %collective-permute-start.1 = (bf16[128,512]{1,0:T(8,128)(2,1)}, bf16[128,512]{1,0:T(8,128)(2,1)S(1)}, u32[]{:S(2)}, u32[]{:S(2)}) collective-permute-start(bf16[128,512]{1,0:T(8,128)(2,1)} %v_hbm.1), channel_id=1, source_target_pairs={{0,2},{2,4},{4,6},{6,8},{8,10},{10,12},{12,14},{14,15},{15,13},{13... | collective-permute-start | bytes 393224 | tf_op jit(solution)/shard_map/ppermute | solution.py:321

commit v9 on v7

--- a/solution.py
+++ b/solution.py
@@ -14,7 +14,7 @@
 EPSILON = 1e-06
 PAIR = 2
 LAG = 1
-STORE_AFTER = (0, 2, 5, 8, 11, 13)
+STORE_AFTER = (0, 1, 3, 6, 9, 12, 14)
 VMEM_LIMIT = 16 * 1024 * 1024
 
 

time: 10.6 us -> 10.6 us (level)
  no operation moved by 1% of the time
where the time goes in v9:
time: 10.6 us; the launch traced here: 10.4 us
  Pallas kernels  5.13 us (48%)
  starting transfers between devices  3.04 us (29%)
  waiting for transfers between devices  2.24 us (21%)
    pallas_call x1, Pallas kernels, local(): pl.pallas_call(functools.partial(local_kernel, cycle, span), in_specs=[hb...  2.79 us
    ppermute x1, waiting for transfers between devices, local(): lax.ppermute(key_proj, ('blk', 'uly'), route)  1.91 us
    ppermute x1, starting transfers between devices, local(): lax.ppermute(key_proj, ('blk', 'uly'), route)  1.55 us
    ppermute x1, starting transfers between devices, local(): lax.ppermute(value_projection, ('blk', 'uly'), route)  1.49 us
    pallas_call x1, Pallas kernels, local(): pl.pallas_call(functools.partial(mix_kernel, cycle), in_specs=[vmem] * (3...  1.27 us
    pallas_call x1, Pallas kernels, local(): pl.pallas_call(functools.partial(weight_kernel, cycle, span), in_specs=[v...  1.07 us
    ppermute x1, waiting for transfers between devices, local(): lax.ppermute(value_projection, ('blk', 'uly'), route)  0.33 us
  transfers between devices with their start and end apart: 2, of which 2 were waited for; matrix products, arithmetic and copies ran while one was open for 0% of the time, Pallas kernels for 37%

profile of v9, /device:TPU:6, one launch (start us, length us, event | category | flops | bytes accessed | tf_op | source)
XLA Modules:
  0.0 10.4 jit_solution(9639179510799352000)
XLA Ops:
  0.0 1.5 %collective-permute-start = (bf16[128,512]{1,0:T(8,128)(2,1)}, bf16[128,512]{1,0:T(8,128)(2,1)S(1)}, u32[]{:S(2)}, u32[]{:S(2)}) collective-permute-start(bf16[128,512]{1,0:T(8,128)(2,1)} %k_hbm.1), channel_id=1, source_target_pairs={{0,2},{2,4},{4,6},{6,8},{8,10},{10,12},{12,14},{14,15},{15,13},{13... | collective-permute-start | bytes 393224 | tf_op jit(solution)/shard_map/ppermute | solution.py:318
  1.5 1.5 %collective-permute-start.1 = (bf16[128,512]{1,0:T(8,128)(2,1)}, bf16[128,512]{1,0:T(8,128)(2,1)S(1)}, u32[]{:S(2)}, u32[]{:S(2)}) collective-permute-start(bf16[128,512]{1,0:T(8,128)(2,1)} %v_hbm.1), channel_id=1, source_target_pairs={{0,2},{2,4},{4,6},{6,8},{8,10},{10,12},{12,14},{14,15},{15,13},{13... | collective-permute-start | bytes 393224 | tf_op jit(solution)/shard_map/ppermute | solution.py:319
  3.0 2.8 %local_scores.1 = (bf16[32,128,128]{2,1,0:T(8,128)(2,1)S(1)}, f32[16,128,256]{2,1,0:T(8,128)S(1)}, f32[1,2,128,128]{3,2,1,0:T(8,128)S(1)}, bf16[4,128,128]{2,1,0:T(8,128)(2,1)S(1)}, bf16[128,4096]{1,0:T(8,128)(2,1)}) custom-call(bf16[128,4096]{1,0:T(8,128)(2,1)} %q_hbm.1, bf16[128,512]{1,0:T(8,128)(2,1)} %k_hbm.1, bf16[128,512]{1,0:T(8,128)(2,1)} %v_hbm.1, ...), custom_call_target="tpu_custom_call" | custom-call | tf_op jit(solution)/shard_map/local_scores/pallas_call | solution.py:323
  5.8 1.9 %collective-permute-done.refs_3_ = bf16[128,512]{1,0:T(8,128)(2,1)S(1)} collective-permute-done((bf16[128,512]{1,0:T(8,128)(2,1)}, bf16[128,512]{1,0:T(8,128)(2,1)S(1)}, u32[]{:S(2)}, u32[]{:S(2)}) %collective-permute-start) | collective-permute-done | bytes 131104 | tf_op jit(solution)/shard_map/ppermute | solution.py:318
  7.8 1.1 %weights.1 = (bf16[16,256,256]{2,1,0:T(8,128)(2,1)S(1)}, f32[16,1,256]{2,1,0:T(1,128)S(1)}) custom-call(bf16[32,128,128]{2,1,0:T(8,128)(2,1)S(1)} %get-tuple-element.12.refs_0_, f32[16,128,256]{2,1,0:T(8,128)S(1)} %get-tuple-element.13.refs_1_, f32[1,2,128,128]{3,2,1,0:T(8,128)S(1)} %get-tuple-element.14.refs_2_, ...), custom_call_target="tpu_custom_call" | custom-call | tf_op jit(solution)/shard_map/weights/pallas_call | solution.py:351
  8.8 0.3 %collective-permute-done.1.refs_0_ = bf16[128,512]{1,0:T(8,128)(2,1)S(1)} collective-permute-done((bf16[128,512]{1,0:T(8,128)(2,1)}, bf16[128,512]{1,0:T(8,128)(2,1)S(1)}, u32[]{:S(2)}, u32[]{:S(2)}) %collective-permute-start.1) | collective-permute-done | bytes 131104 | tf_op jit(solution)/shard_map/ppermute | solution.py:319
  9.2 1.3 %mix_values.1 = bf16[128,4096]{1,0:T(8,128)(2,1)} custom-call(bf16[16,256,256]{2,1,0:T(8,128)(2,1)S(1)} %get-tuple-element.15.weight_ref, f32[16,1,256]{2,1,0:T(1,128)S(1)} %get-tuple-element.16.inverse_ref, bf16[4,128,128]{2,1,0:T(8,128)(2,1)S(1)} %get-tuple-element.17.own_value_ref, ...), custom_call_target="tpu_custom_call", output_to_operand_aliasing={{}: (4, {})} | custom-call | tf_op jit(solution)/shard_map/mix_values/pallas_call | solution.py:362
Async XLA Ops:
  0.0 7.8 %collective-permute-start = (bf16[128,512]{1,0:T(8,128)(2,1)}, bf16[128,512]{1,0:T(8,128)(2,1)S(1)}, u32[]{:S(2)}, u32[]{:S(2)}) collective-permute-start(bf16[128,512]{1,0:T(8,128)(2,1)} %k_hbm.1), channel_id=1, source_target_pairs={{0,2},{2,4},{4,6},{6,8},{8,10},{10,12},{12,14},{14,15},{15,13},{13... | collective-permute-start | bytes 393224 | tf_op jit(solution)/shard_map/ppermute | solution.py:318
  1.5 7.6 %collective-permute-start.1 = (bf16[128,512]{1,0:T(8,128)(2,1)}, bf16[128,512]{1,0:T(8,128)(2,1)S(1)}, u32[]{:S(2)}, u32[]{:S(2)}) collective-permute-start(bf16[128,512]{1,0:T(8,128)(2,1)} %v_hbm.1), channel_id=1, source_target_pairs={{0,2},{2,4},{4,6},{6,8},{8,10},{10,12},{12,14},{14,15},{15,13},{13... | collective-permute-start | bytes 393224 | tf_op jit(solution)/shard_map/ppermute | solution.py:319
